TPU v7x, 32 devices: a whole 2x2x4 slice. The times are simulated.
32 devices in a mesh: groups: 2 (over x), query: 16 (over z, y, core).
Axes of the slice: x: 2, y: 2, z: 4, core: 2. Of those that a mesh axis runs over, the one named last changes fastest.
Arguments:
- tokens: bfloat16 [384, 4096], P(('groups', 'query')), parts along dimension 0, may hold values from -6 to 6
- grad_out: bfloat16 [384, 4096], P(('groups', 'query')), parts along dimension 0, may hold values from -6 to 6
- gate_weight: bfloat16 [4096, 14336], P(None, 'query'), may hold values from -0.09375 to 0.09375
- up_weight: bfloat16 [4096, 14336], P(None, 'query'), may hold values from -0.09375 to 0.09375
- query_left: bfloat16 [16, 4096, 32], P('query'), may hold values from -0.09375 to 0.09375
- query_right: bfloat16 [16, 14336, 32], P('query'), may hold values from -0.09375 to 0.09375
Outputs:
- scores: float32 [384, 16], P(('groups', 'query')), parts along dimension 0
There are 2 independent parts, one for each index of `groups`. A program takes and returns all parts, laid end to end along the dimension named above; an argument that names none is the same for every part. Nothing has to cross between parts.
All inputs are finite; a program needn't handle non-finite values.
Results may differ from a plain program's by a relative error of at most 0.0003.
Values may be sent and summed in bfloat16 or wider, within the bound.
No kernel may reach another device: no remote copies, remote signals or barrier semaphores. Data moves between devices by JAX's collectives and lax.ppermute only.
A program may use at most 128 MiB of HBM per device.

v0:
```python
import jax
import jax.numpy as jnp
from jax import lax
from jax.sharding import PartitionSpec as P


def body(tokens, grad_out, gate_weight, up_weight, query_left, query_right):
    whole = lax.all_gather(tokens, "query", axis=0, tiled=True)
    right_cols = lax.all_to_all(query_right, "query", split_axis=1, concat_axis=0, tiled=True)
    right_wide = right_cols.astype(jnp.float32)
    num_queries = right_cols.shape[0]
    rank_size = right_cols.shape[2]
    tok_rows = tokens.shape[0]
    gate = jnp.dot(whole, gate_weight, preferred_element_type=jnp.float32)
    up = jnp.dot(whole, up_weight, preferred_element_type=jnp.float32)
    hidden = jax.nn.silu(gate) * up
    term = jnp.einsum("tf,qfr->tqr", hidden, right_wide, precision=lax.Precision.HIGHEST)
    proj_right = lax.psum_scatter(
        term.reshape(tok_rows * lax.axis_size("query"), num_queries * rank_size),
        "query",
        scatter_dimension=0,
        tiled=True,
    )
    proj_right = proj_right.reshape(tok_rows, num_queries, rank_size)
    left = jnp.einsum(
        "td,kdr->tkr",
        grad_out,
        lax.all_gather(query_left, "query", axis=0, tiled=True),
        preferred_element_type=jnp.float32,
    )
    return jnp.sum(left * proj_right, axis=2)


def solution(mesh):
    return jax.shard_map(
        body,
        mesh=mesh,
        in_specs=(
            P(("groups", "query"), None),
            P(("groups", "query"), None),
            P(None, "query"),
            P(None, "query"),
            P("query", None, None),
            P("query", None, None),
        ),
        out_specs=P(("groups", "query"), None),
        check_vma=False,
    )
```

profile of v0, /device:TPU:0, one launch (start us, length us, event | category | flops | bytes accessed | tf_op | source)
XLA Modules:
  0.0 229.4 jit_solution(11249629762622206637)
XLA Ops:
  6.5 0.0 copy-start
  6.5 0.0 all-gather.6.cloned.1.call-start
  6.5 0.7 all-gather.6.cloned.1.call-update
  7.3 0.0 all-gather.4.cloned.1.call-start
  7.3 0.7 all-gather.4.cloned.1.call-update
  8.0 14.3 %copy.10 = bf16[1,14336,32]{2,0,1:T(2,128)(2,1)} copy(bf16[1,14336,32]{1,2,0:T(8,128)(2,1)} %param.11) | data formatting | bytes 1835008 | tf_op args[5]
  22.3 0.5 broadcast.2
  22.8 79.8 %reduce = bf16[14336,32]{1,0:T(8,128)(2,1)} reduce(bf16[14336,1,32]{2,1,0:T(2,128)(2,1)} %bitcast.26, bf16[]{:T(256)} %broadcast.2), dimensions={1}, to_apply=%bitcast.15.reduce_sub_computation | reduce | bytes 1835010
  102.6 5.0 %reshape.13 = bf16[16,2,14336]{2,1,0:T(2,128)(2,1)S(1)} reshape(bf16[14336,32]{1,0:T(8,128)(2,1)} %reduce) | data formatting | bytes 1835008
  107.5 29.8 %all_to_all.12 = bf16[16,2,14336]{2,1,0:T(2,128)(2,1)S(1)} all-to-all(bf16[16,2,14336]{2,1,0:T(2,128)(2,1)S(1)} %reshape.13), channel_id=1, replica_groups=mesh['groups'=2,'query'=16] {'query'}, dimensions={0} | all-to-all | bytes 1835008 | tf_op jit(solution)/shard_map/all_to_all | solution.py:9
  137.3 8.4 %reshape.14 = bf16[14336,1,32]{2,1,0:T(2,128)(2,1)} reshape(bf16[16,2,14336]{2,1,0:T(2,128)(2,1)S(1)} %all_to_all.12) | data formatting | bytes 1835008
  145.6 13.7 %copy.11 = bf16[1,14336,32]{1,2,0:T(8,128)(2,1)S(1)} copy(bf16[1,14336,32]{2,0,1:T(2,128)(2,1)} %bitcast.27) | data formatting | bytes 1835008 | tf_op jit(solution)/shard_map/all_to_all | solution.py:9
  159.3 0.1 copy.15
  159.4 0.2 copy.12
  159.6 0.0 all-gather.6.cloned.1.call-done
  159.6 2.5 %reshape.10 = bf16[192,4096]{1,0:T(8,128)(2,1)S(1)} reshape(bf16[16,12,4096]{2,1,0:T(8,128)(2,1)} %all-gather.6.cloned.1.call-done) | data formatting | bytes 3145728
  162.1 4.9 %fusion.4 = f32[192,896]{1,0:T(8,128)S(1)} fusion(bf16[192,4096]{1,0:T(8,128)(2,1)S(1)} %reshape.10, bf16[4096,896]{1,0:T(8,128)(2,1)} %param.8), kind=kOutput, calls=%fused_computation.6 | convolution fusion | flops 1409286144 | bytes 9601024 | tf_op jit(solution)/shard_map/dot_general | solution.py:14
  167.0 0.0 copy-start.1
  167.0 4.9 %convolution_multiply_fusion = f32[192,896]{1,0:T(8,128)S(1)} fusion(bf16[192,4096]{1,0:T(8,128)(2,1)S(1)} %reshape.10, bf16[4096,896]{1,0:T(8,128)(2,1)} %param.9, f32[192,896]{1,0:T(8,128)S(1)} %fusion.4), kind=kOutput, calls=%fused_computation | convolution fusion | flops 1410146304 | bytes 10289152 | tf_op jit(solution)/shard_map/dot_general | solution.py:15
  171.9 1.1 fusion.5
  173.0 36.3 %fusion = f32[16,512]{1,0:T(8,128)S(1)} fusion(f32[192,512]{1,0:T(8,128)S(1)} %fusion.5), kind=kCustom, calls=%all-reduce-scatter | all-reduce-scatter fusion | flops 131073 | bytes 426496
  209.3 1.3 collective-permute-start
  210.6 1.3 collective-permute-start.1
  211.9 1.3 collective-permute-start.2
  213.3 1.3 collective-permute-start.3
  214.6 0.0 copy-done.1
  214.6 0.6 dynamic-slice.4
  215.8 0.3 collective-permute-done.3
  216.1 0.0 collective-permute-done
  216.1 0.0 collective-permute-done.1
  216.1 0.0 collective-permute-done.2
  216.2 0.5 concatenate
  216.7 0.1 reshape.8
  216.8 0.0 all-gather.4.cloned.1.call-done
  216.8 0.0 copy-done
  216.8 5.1 %fusion.3 = f32[12,16]{0,1:T(8,128)S(1)} fusion(f32[12,16,32]{2,1,0:T(8,128)S(1)} %reshape.8, bf16[16,4096,32]{1,2,0:T(8,128)(2,1)} %all-gather.4.cloned.1.call-done, bf16[12,4096]{1,0:T(8,128)(2,1)S(1)} %copy-done), kind=kOutput, calls=%fused_computation.4 | convolution fusion | flops 50343744 | bytes 4317952 | tf_op jit(solution)/shard_map/td,kdr->tkr/dot_general | solution.py:25
  221.9 0.7 copy.14
  (2 shorter events, 0.0 us)
Async XLA Ops:
  6.5 210.3 %copy-start = (bf16[12,4096]{1,0:T(8,128)(2,1)S(1)}, bf16[12,4096]{1,0:T(8,128)(2,1)}, u32[]{:S(2)}) copy-start(bf16[12,4096]{1,0:T(8,128)(2,1)} %param.7) | copy-start | bytes 294916
  6.5 153.1 %all-gather.6.cloned.1.call-start = ((), (), s32[]{:S(2)}) async-start(), calls=%async_computation.2 | async-start | bytes 2228224 | tf_op jit(solution)/shard_map/all_gather | solution.py:8
  7.3 209.5 %all-gather.4.cloned.1.call-start = ((), (), s32[]{:S(2)}) async-start(), calls=%async_computation.1 | async-start | bytes 4456448 | tf_op jit(solution)/shard_map/all_gather | solution.py:28
  167.0 47.6 %copy-start.1 = (u32[32]{0:T(128)S(1)}, u32[32]{0:T(128)}, u32[]{:S(2)}) copy-start(u32[32]{0:T(128)} %constant.11) | copy-start | bytes 388
  209.3 6.8 %collective-permute-start = (f32[16,512]{1,0:T(8,128)S(1)}, f32[16,512]{1,0:T(8,128)S(1)}, u32[]{:S(2)}, u32[]{:S(2)}) collective-permute-start(f32[16,512]{1,0:T(8,128)S(1)} %fusion), channel_id=1, source_target_pairs={{0,1},{1,2},{2,3},{3,4},{4,5},{5,6},{6,7},{7,8},{8,9},{9,10},{10,1... | collective-permute-start | bytes 98312
  210.6 5.5 %collective-permute-start.1 = (f32[16,512]{1,0:T(8,128)S(1)}, f32[16,512]{1,0:T(8,128)S(1)}, u32[]{:S(2)}, u32[]{:S(2)}) collective-permute-start(f32[16,512]{1,0:T(8,128)S(1)} %fusion), channel_id=1, source_target_pairs={{0,2},{1,3},{2,4},{3,5},{4,6},{5,7},{6,8},{7,9},{8,10},{9,11},{10,... | collective-permute-start | bytes 98312
  211.9 4.2 %collective-permute-start.2 = (f32[16,512]{1,0:T(8,128)S(1)}, f32[16,512]{1,0:T(8,128)S(1)}, u32[]{:S(2)}, u32[]{:S(2)}) collective-permute-start(f32[16,512]{1,0:T(8,128)S(1)} %fusion), channel_id=1, source_target_pairs={{0,3},{1,4},{2,5},{3,6},{4,7},{5,8},{6,9},{7,10},{8,11},{9,12},{10... | collective-permute-start | bytes 98312
  213.3 2.9 %collective-permute-start.3 = (f32[12,512]{1,0:T(8,128)S(1)}, f32[12,512]{1,0:T(8,128)S(1)}, u32[]{:S(2)}, u32[]{:S(2)}) collective-permute-start(f32[12,512]{1,0:T(8,128)S(1)} %slice), channel_id=1, source_target_pairs={{0,4},{1,5},{2,6},{3,7},{4,8},{5,9},{6,10},{7,11},{8,12},{9,13},{1... | collective-permute-start | bytes 73736
Sparse Core Ops, SparseCore 0:
  9.5 44.0 all-gather.5
  55.8 49.4 all-gather.3
where the time goes:
time: 232 us; the launch traced here: 229 us
  other arithmetic  79.8 us (34%)
  blocking collectives  66.1 us (28%)
  local copies, waits for them, and re-layouts  46.4 us (20%)
  matrix products  16 us (7%)
  between operations  14.2 us (6%)
  starting transfers between devices  5.21 us (2%)
    unnamed x1, other arithmetic  79.8 us
    unnamed x1, blocking collectives  36.3 us
    unnamed x14, local copies, waits for them, and re-layouts  31.8 us
    all_to_all x1, blocking collectives, body(): lax.all_to_all(query_right, 'query', split_axis=1, concat_axis=0, tiled=T...  29.8 us
    all_to_all x1, local copies, waits for them, and re-layouts, body(): lax.all_to_all(query_right, 'query', split_axis=1, concat_axis=0, tiled=T...  13.7 us
    unnamed x4, starting transfers between devices  5.17 us
    dot_general x1, matrix products, body(): jnp.einsum('td,kdr->tkr', grad_out, lax.all_gather(query_left, 'query', a...  5.07 us
    dot_general x1, matrix products, body(): up = jnp.dot(whole, up_weight, preferred_element_type=jnp.float32)  4.93 us
  transfers between devices with their start and end apart: 6, of which 1 were waited for; matrix products, arithmetic and copies ran while one was open for 75% of the time, Pallas kernels for 0%

commit v1 on v0

v1 whole, which is shorter than its diff:
```python
import jax
import jax.numpy as jnp
from jax import lax
from jax.sharding import PartitionSpec as P

AXIS = "query"
F32 = jnp.float32
BF16 = jnp.bfloat16


def swap(x, bit):
    n = lax.axis_size(AXIS)
    return lax.ppermute(x, AXIS, [(i, i ^ bit) for i in range(n)])


def pick(flag, when_zero, when_one):
    return jnp.where(flag == 0, when_zero, when_one)


def z_order(planes):
    order = [0]
    bit = planes // 2
    while bit >= 1:
        order = order + [k | bit for k in order]
        bit //= 2
    return order


def gather_rows(rows, core, planes):
    half = rows.shape[1] // 2
    mine = pick(core, rows[:, :half], rows[:, half:])
    theirs = pick(core, rows[:, half:], rows[:, :half])
    other = swap(theirs, 1)
    chip = pick(core, jnp.concatenate([mine, other]), jnp.concatenate([other, mine]))
    column = jnp.concatenate([chip if k == 0 else swap(chip, 4 * k) for k in z_order(planes)])
    both = jnp.concatenate([column, swap(column, 2)])
    rest = swap(both, 1)
    return pick(core, jnp.concatenate([both, rest], 1), jnp.concatenate([rest, both], 1))


def body(tokens, grad_out, gate_weight, up_weight, query_left, query_right):
    n = lax.axis_size(AXIS)
    planes = n // 4
    here = lax.axis_index(AXIS)
    core, y, z = here & 1, (here >> 1) & 1, here >> 2
    rank = query_right.shape[2]
    cols = gate_weight.shape[1]

    blocks = query_right[0].T.reshape(rank, n, cols).transpose(1, 0, 2)
    factors = lax.all_to_all(blocks, AXIS, split_axis=0, concat_axis=0, tiled=True)
    factors = factors.reshape(n // 2, 2, rank, cols)
    keep_factors = pick(core, factors[:, 0], factors[:, 1]).reshape(n // 2 * rank, cols)
    send_factors = pick(core, factors[:, 1], factors[:, 0]).reshape(n // 2 * rank, cols)

    whole = gather_rows(tokens, core, planes)
    grads = gather_rows(grad_out, core, planes)

    gate = jnp.dot(whole, gate_weight, preferred_element_type=F32)
    up = jnp.dot(whole, up_weight, preferred_element_type=F32)
    hidden = jax.nn.silu(gate) * up
    head = lax.reduce_precision(hidden, exponent_bits=8, mantissa_bits=7)
    high = head.astype(BF16)
    low = (hidden - head).astype(BF16)

    def project(with_factors):
        dims = (((1,), (1,)), ((), ()))
        return lax.dot_general(high, with_factors, dims, preferred_element_type=F32) + lax.dot_general(
            low, with_factors, dims, preferred_element_type=F32
        )

    left = jnp.dot(grads, query_left[0], preferred_element_type=F32)
    right = project(keep_factors) + swap(project(send_factors), 1)

    bit, place = 2, y
    while bit < n:
        half = right.shape[0] // 2
        right = right[:half] + swap(right[half:], bit)
        other = swap(left[half:], bit)
        left = pick(place, jnp.concatenate([left[:half], other], 1), jnp.concatenate([other, left[:half]], 1))
        bit *= 2
        place = (here // bit) & 1

    own = tokens.shape[0]
    spread = lax.broadcasted_iota(jnp.int32, (n // 2 * rank, n), 0) // rank * 2 + core
    spread = (spread == lax.broadcasted_iota(jnp.int32, (n // 2 * rank, n), 1)).astype(F32)
    sums = jnp.dot(left * right, spread, precision=lax.Precision.HIGHEST)
    return pick(core, sums[:own], sums[own:]) + swap(pick(core, sums[own:], sums[:own]), 1)


def solution(mesh):
    return jax.shard_map(
        body,
        mesh=mesh,
        in_specs=(
            P(("groups", "query"), None),
            P(("groups", "query"), None),
            P(None, "query"),
            P(None, "query"),
            P("query", None, None),
            P("query", None, None),
        ),
        out_specs=P(("groups", "query"), None),
        check_vma=False,
    )
```

time: 232 us -> 86.3 us (0.37); the launches traced: 229 us -> 86 us
  other arithmetic: 79.8 us -> 2.38 us
  blocking collectives: 66.1 us -> 0 us
  local copies, waits for them, and re-layouts: 46.4 us -> 2.3 us
  starting transfers between devices: 5.21 us -> 41.8 us
  waiting for transfers between devices: 1.79 us -> 28.6 us
  between operations: 14.2 us -> 0.29 us
  matrix products: 16 us -> 10.7 us
    unnamed x1 -> x3, other arithmetic: 79.8 us -> 0.11 us
    unnamed x1 -> x0, blocking collectives: 36.3 us -> none
    ppermute x0 -> x20, starting transfers between devices: none -> 33.7 us  [swap(): return lax.ppermute(x, AXIS, [(i, i ^ bit) for i in range(n)])]
    unnamed x14 -> x15, local copies, waits for them, and re-layouts: 31.8 us -> 0.16 us
    all_to_all x1 -> x0, blocking collectives: 29.8 us -> none  [body(): lax.all_to_all(query_right, 'query', split_axis=1, concat_axis=0, tiled=T...]
    ppermute x0 -> x20, waiting for transfers between devices: none -> 24.2 us  [swap(): return lax.ppermute(x, AXIS, [(i, i ^ bit) for i in range(n)])]
    all_to_all x1 -> x0, local copies, waits for them, and re-layouts: 13.7 us -> none  [body(): lax.all_to_all(query_right, 'query', split_axis=1, concat_axis=0, tiled=T...]
    all_to_all x0 -> x1, starting transfers between devices: none -> 8.12 us  [body(): lax.all_to_all(blocks, AXIS, split_axis=0, concat_axis=0, tiled=True)]
  transfers between devices with their start and end apart: 6 -> 21, of which waited for: 1 -> 10; matrix products, arithmetic and copies ran while one was open for 75% -> 14% of each run, Pallas kernels for 0% -> 0%
where the time goes in v1:
time: 86.3 us; the launch traced here: 86 us
  starting transfers between devices  41.8 us (48%)
  waiting for transfers between devices  28.6 us (33%)
  matrix products  10.7 us (12%)
  other arithmetic  2.38 us (3%)
  local copies, waits for them, and re-layouts  2.3 us (3%)
    ppermute x20, starting transfers between devices, swap(): return lax.ppermute(x, AXIS, [(i, i ^ bit) for i in range(n)])  33.7 us
    ppermute x20, waiting for transfers between devices, swap(): return lax.ppermute(x, AXIS, [(i, i ^ bit) for i in range(n)])  24.2 us
    all_to_all x1, starting transfers between devices, body(): lax.all_to_all(blocks, AXIS, split_axis=0, concat_axis=0, tiled=True)  8.12 us
    dot_general x1, matrix products, body(): gate = jnp.dot(whole, gate_weight, preferred_element_type=F32)  5.16 us
    all_to_all x1, waiting for transfers between devices, body(): lax.all_to_all(blocks, AXIS, split_axis=0, concat_axis=0, tiled=True)  4.41 us
    select_n x6, other arithmetic, pick(): return jnp.where(flag == 0, when_zero, when_one)  2.12 us
    dot_general x1, matrix products, body(): left = jnp.dot(grads, query_left[0], preferred_element_type=F32)  1.97 us
    dot_general x1, matrix products, body(): up = jnp.dot(whole, up_weight, preferred_element_type=F32)  1.87 us
  transfers between devices with their start and end apart: 21, of which 10 were waited for; matrix products, arithmetic and copies ran while one was open for 14% of the time, Pallas kernels for 0%

profile of v1, /device:TPU:0, one launch (start us, length us, event | category | flops | bytes accessed | tf_op | source)
XLA Modules:
  0.0 86.0 jit_solution(18113915444369536713)
XLA Ops:
  0.0 1.0 %broadcast_select_fusion.4 = (bf16[12,2048]{1,0:T(8,128)(2,1)S(1)}, bf16[12,2048]{1,0:T(8,128)(2,1)S(1)}) fusion(pred[]{:T(512)S(6)} %eq.10, bf16[12,4096]{1,0:T(8,128)(2,1)} %param.7), kind=kLoop, calls=%fused_computation.37 | loop fusion | flops 49152 | bytes 196609 | tf_op jit(solution)/shard_map/jit(_where)/select_n | solution.py:17
  1.0 0.5 collective-permute-start
  1.5 0.9 %broadcast_select_fusion.2 = (bf16[12,2048]{1,0:T(8,128)(2,1)S(1)}, bf16[12,2048]{1,0:T(8,128)(2,1)S(1)}) fusion(pred[]{:T(512)S(6)} %eq.10, bf16[12,4096]{1,0:T(8,128)(2,1)} %param.6), kind=kLoop, calls=%fused_computation.35 | loop fusion | flops 49152 | bytes 196609 | tf_op jit(solution)/shard_map/jit(_where)/select_n | solution.py:17
  2.4 0.1 collective-permute-start.9
  2.6 4.1 %collective-permute-start.1 = (bf16[24,2048]{1,0:T(8,128)(2,1)S(1)}, bf16[24,2048]{1,0:T(8,128)(2,1)S(1)}, u32[]{:S(2)}, u32[]{:S(2)}) collective-permute-start(bf16[24,2048]{1,0:T(8,128)(2,1)S(1)} %get-tuple-element.6), channel_id=1, source_target_pairs={{0,8},{1,9},{2,10},{3,11},{4,12},{5,13},{6,14},{7,15},{8,0},{9,1},... | collective-permute-start | bytes 294920 | tf_op jit(solution)/shard_map/ppermute | solution.py:13
  6.7 1.6 %collective-permute-start.2 = (bf16[24,2048]{1,0:T(8,128)(2,1)S(1)}, bf16[24,2048]{1,0:T(8,128)(2,1)S(1)}, u32[]{:S(2)}, u32[]{:S(2)}) collective-permute-start(bf16[24,2048]{1,0:T(8,128)(2,1)S(1)} %get-tuple-element.6), channel_id=1, source_target_pairs={{0,4},{1,5},{2,6},{3,7},{4,0},{5,1},{6,2},{7,3},{8,12},{9,13},{10,... | collective-permute-start | bytes 294920 | tf_op jit(solution)/shard_map/ppermute | solution.py:13
  8.3 2.0 %collective-permute-start.10 = (bf16[24,2048]{1,0:T(8,128)(2,1)S(1)}, bf16[24,2048]{1,0:T(8,128)(2,1)S(1)}, u32[]{:S(2)}, u32[]{:S(2)}) collective-permute-start(bf16[24,2048]{1,0:T(8,128)(2,1)S(1)} %get-tuple-element.8), channel_id=1, source_target_pairs={{0,8},{1,9},{2,10},{3,11},{4,12},{5,13},{6,14},{7,15},{8,0},{9,1},... | collective-permute-start | bytes 294920 | tf_op jit(solution)/shard_map/ppermute | solution.py:13
  10.3 2.5 %collective-permute-start.11 = (bf16[24,2048]{1,0:T(8,128)(2,1)S(1)}, bf16[24,2048]{1,0:T(8,128)(2,1)S(1)}, u32[]{:S(2)}, u32[]{:S(2)}) collective-permute-start(bf16[24,2048]{1,0:T(8,128)(2,1)S(1)} %get-tuple-element.8), channel_id=1, source_target_pairs={{0,4},{1,5},{2,6},{3,7},{4,0},{5,1},{6,2},{7,3},{8,12},{9,13},{10,... | collective-permute-start | bytes 294920 | tf_op jit(solution)/shard_map/ppermute | solution.py:13
  12.8 6.2 %collective-permute-start.12 = (bf16[24,2048]{1,0:T(8,128)(2,1)S(1)}, bf16[24,2048]{1,0:T(8,128)(2,1)S(1)}, u32[]{:S(2)}, u32[]{:S(2)}) collective-permute-start(bf16[24,2048]{1,0:T(8,128)(2,1)S(1)} %get-tuple-element.8), channel_id=1, source_target_pairs={{0,12},{1,13},{2,14},{3,15},{4,8},{5,9},{6,10},{7,11},{8,4},{9,5},... | collective-permute-start | bytes 294920 | tf_op jit(solution)/shard_map/ppermute | solution.py:13
  19.0 1.6 %collective-permute-start.4 = (bf16[96,2048]{1,0:T(8,128)(2,1)S(1)}, bf16[96,2048]{1,0:T(8,128)(2,1)S(1)}, u32[]{:S(2)}, u32[]{:S(2)}) collective-permute-start(bf16[96,2048]{1,0:T(8,128)(2,1)S(1)} %pad_maximum_fusion), channel_id=1, source_target_pairs={{0,2},{1,3},{2,0},{3,1},{4,6},{5,7},{6,4},{7,5},{8,10},{9,11},{10,... | collective-permute-start | bytes 1179656 | tf_op jit(solution)/shard_map/ppermute | solution.py:13
  20.6 2.3 %collective-permute-done.10 = bf16[24,2048]{1,0:T(8,128)(2,1)S(1)} collective-permute-done((bf16[24,2048]{1,0:T(8,128)(2,1)S(1)}, bf16[24,2048]{1,0:T(8,128)(2,1)S(1)}, u32[]{:S(2)}, u32[]{:S(2)}) %collective-permute-start.10) | collective-permute-done | bytes 98336 | tf_op jit(solution)/shard_map/ppermute | solution.py:13
  23.0 1.9 %collective-permute-start.13 = (bf16[96,2048]{1,0:T(8,128)(2,1)S(1)}, bf16[96,2048]{1,0:T(8,128)(2,1)S(1)}, u32[]{:S(2)}, u32[]{:S(2)}) collective-permute-start(bf16[96,2048]{1,0:T(8,128)(2,1)S(1)} %pad_maximum_fusion.1), channel_id=1, source_target_pairs={{0,2},{1,3},{2,0},{3,1},{4,6},{5,7},{6,4},{7,5},{8,10},{9,11},{10,... | collective-permute-start | bytes 1179656 | tf_op jit(solution)/shard_map/ppermute | solution.py:13
  24.9 4.9 %collective-permute-done.4 = bf16[96,2048]{1,0:T(8,128)(2,1)S(1)} collective-permute-done((bf16[96,2048]{1,0:T(8,128)(2,1)S(1)}, bf16[96,2048]{1,0:T(8,128)(2,1)S(1)}, u32[]{:S(2)}, u32[]{:S(2)}) %collective-permute-start.4) | collective-permute-done | bytes 393248 | tf_op jit(solution)/shard_map/ppermute | solution.py:13
  29.8 0.1 collective-permute-start.5
  29.9 5.5 %collective-permute-done.13 = bf16[96,2048]{1,0:T(8,128)(2,1)S(1)} collective-permute-done((bf16[96,2048]{1,0:T(8,128)(2,1)S(1)}, bf16[96,2048]{1,0:T(8,128)(2,1)S(1)}, u32[]{:S(2)}, u32[]{:S(2)}) %collective-permute-start.13) | collective-permute-done | bytes 393248 | tf_op jit(solution)/shard_map/ppermute | solution.py:13
  35.4 0.1 collective-permute-start.14
  35.5 0.1 copy.34
  35.6 1.1 %copy.32 = bf16[16,32,896]{2,1,0:T(8,128)(2,1)} copy(bf16[16,32,896]{2,0,1:T(8,128)(2,1)S(1)} %bitcast.23) | data formatting | bytes 1835008 | tf_op jit(solution)/shard_map/transpose | solution.py:49
  36.7 8.1 %all-to-all-start = ((bf16[16,32,896]{2,1,0:T(8,128)(2,1)}), bf16[16,32,896]{2,1,0:T(8,128)(2,1)S(1)}, u32[]{:S(2)}, u32[]{:S(2)}) async-start(bf16[16,32,896]{2,1,0:T(8,128)(2,1)} %copy.32), calls=%async_computation | async-start | bytes 1835008 | tf_op jit(solution)/shard_map/all_to_all | solution.py:50
  44.9 2.0 %fusion = f32[192,32]{0,1:T(8,128)S(1)} fusion(bf16[192,2048]{1,0:T(8,128)(2,1)} %collective-permute-done.5, bf16[192,2048]{1,0:T(8,128)(2,1)S(1)} %constant_dynamic-update-slice_fusion, pred[]{:T(512)S(6)} %eq.10, bf16[1,4096,32]{1,2,0:T(8,128)(2,1)S(1)} %copy-done), kind=kOutput, calls=%fused_computation.1 | convolution fusion | flops 57409536 | bytes 1859585 | tf_op jit(solution)/shard_map/dot_general | solution.py:71
  46.9 0.1 fusion.36
  47.0 1.9 %collective-permute-start.6 = (f32[96,32]{0,1:T(8,128)S(1)}, f32[96,32]{0,1:T(8,128)S(1)}, u32[]{:S(2)}, u32[]{:S(2)}) collective-permute-start(f32[96,32]{0,1:T(8,128)S(1)} %get-tuple-element.18), channel_id=1, source_target_pairs={{0,2},{1,3},{2,0},{3,1},{4,6},{5,7},{6,4},{7,5},{8,10},{9,11},{10,... | collective-permute-start | bytes 36872 | tf_op jit(solution)/shard_map/ppermute | solution.py:13
  48.9 5.2 %fusion.10 = f32[192,896]{1,0:T(8,128)S(1)} fusion(bf16[4096,896]{1,0:T(8,128)(2,1)} %param.8, bf16[192,2048]{1,0:T(8,128)(2,1)S(1)} %collective-permute-done.14, bf16[192,2048]{1,0:T(8,128)(2,1)S(1)} %constant_dynamic-update-slice_fusion.5, pred[]{:T(512)S(6)} %eq.10), kind=kOutput, calls=%fused_computation.21 | convolution fusion | flops 1416364032 | bytes 9601025 | tf_op jit(solution)/shard_map/dot_general | solution.py:58
  54.1 0.1 fusion.35
  54.2 1.9 %collective-permute-start.7 = (f32[48,64]{0,1:T(8,128)S(1)}, f32[48,64]{0,1:T(8,128)S(1)}, u32[]{:S(2)}, u32[]{:S(2)}) collective-permute-start(f32[48,64]{0,1:T(8,128)S(1)} %get-tuple-element.16), channel_id=1, source_target_pairs={{0,4},{1,5},{2,6},{3,7},{4,0},{5,1},{6,2},{7,3},{8,12},{9,13},{10,... | collective-permute-start | bytes 36872 | tf_op jit(solution)/shard_map/ppermute | solution.py:13
  56.1 1.9 %multiply_multiply_fusion = f32[192,896]{1,0:T(8,128)S(1)} fusion(f32[192,896]{1,0:T(8,128)S(1)} %fusion.10, bf16[4096,896]{1,0:T(8,128)(2,1)S(1)} %bitcast.27, bf16[192,2048]{1,0:T(8,128)(2,1)S(1)} %collective-permute-done.14, bf16[192,2048]{1,0:T(8,128)(2,1)S(1)} %constant_dynamic-update-slice_fusion.5, pred[]{:T(512)S(6)} %eq.10), kind=kOutput, calls=%fused_computation.15 | convolution fusion | flops 1417224192 | bytes 10289153 | tf_op jit(solution)/shard_map/dot_general | solution.py:59
  58.0 3.4 %collective-permute-done.7 = f32[48,64]{0,1:T(8,128)S(1)} collective-permute-done((f32[48,64]{0,1:T(8,128)S(1)}, f32[48,64]{0,1:T(8,128)S(1)}, u32[]{:S(2)}, u32[]{:S(2)}) %collective-permute-start.7) | collective-permute-done | bytes 12320 | tf_op jit(solution)/shard_map/ppermute | solution.py:13
  61.5 4.4 %all-to-all-done = bf16[16,32,896]{2,1,0:T(8,128)(2,1)S(1)} async-done(((bf16[16,32,896]{2,1,0:T(8,128)(2,1)}), bf16[16,32,896]{2,1,0:T(8,128)(2,1)S(1)}, u32[]{:S(2)}, u32[]{:S(2)}) %all-to-all-start) | async-done | bytes 917536 | tf_op jit(solution)/shard_map/all_to_all | solution.py:50
  65.9 0.1 broadcast_select_fusion.1
  66.0 0.3 fusion.12
  66.3 0.3 convolution_add_fusion
  66.7 0.2 collective-permute-start.15
  66.9 0.3 fusion.13
  67.2 0.9 %collective-permute-done.15 = f32[192,256]{1,0:T(8,128)S(1)} collective-permute-done((f32[192,256]{1,0:T(8,128)S(1)}, f32[192,256]{1,0:T(8,128)S(1)}, u32[]{:S(2)}, u32[]{:S(2)}) %collective-permute-start.15) | collective-permute-done | bytes 196640 | tf_op jit(solution)/shard_map/ppermute | solution.py:13
  68.2 0.3 fusion.7
  68.5 1.7 %collective-permute-start.16 = (f32[96,256]{1,0:T(8,128)S(1)}, f32[96,256]{1,0:T(8,128)S(1)}, u32[]{:S(2)}, u32[]{:S(2)}) collective-permute-start(f32[96,256]{1,0:T(8,128)S(1)} %slice.100), channel_id=1, source_target_pairs={{0,2},{1,3},{2,0},{3,1},{4,6},{5,7},{6,4},{7,5},{8,10},{9,11},{10,... | collective-permute-start | bytes 294920 | tf_op jit(solution)/shard_map/ppermute | solution.py:13
  70.2 0.1 maximum_select_fusion.10
  70.3 3.2 %collective-permute-done.16 = f32[96,256]{1,0:T(8,128)S(1)} collective-permute-done((f32[96,256]{1,0:T(8,128)S(1)}, f32[96,256]{1,0:T(8,128)S(1)}, u32[]{:S(2)}, u32[]{:S(2)}) %collective-permute-start.16) | collective-permute-done | bytes 98336 | tf_op jit(solution)/shard_map/ppermute | solution.py:13
  73.6 3.0 %collective-permute-start.17 = (f32[48,256]{1,0:T(8,128)S(1)}, f32[48,256]{1,0:T(8,128)S(1)}, u32[]{:S(2)}, u32[]{:S(2)}) collective-permute-start(f32[48,256]{1,0:T(8,128)S(1)} %slice.102), channel_id=1, source_target_pairs={{0,4},{1,5},{2,6},{3,7},{4,0},{5,1},{6,2},{7,3},{8,12},{9,13},{10,... | collective-permute-start | bytes 147464 | tf_op jit(solution)/shard_map/ppermute | solution.py:13
  76.6 1.2 %collective-permute-start.8 = (f32[24,128]{1,0:T(8,128)S(1)}, f32[24,128]{1,0:T(8,128)S(1)}, u32[]{:S(2)}, u32[]{:S(2)}) collective-permute-start(f32[24,128]{1,0:T(8,128)S(1)} %get-tuple-element.20), channel_id=1, source_target_pairs={{0,8},{1,9},{2,10},{3,11},{4,12},{5,13},{6,14},{7,15},{8,0},{9,1},... | collective-permute-start | bytes 36872 | tf_op jit(solution)/shard_map/ppermute | solution.py:13
  77.8 0.9 %collective-permute-done.17 = f32[48,256]{1,0:T(8,128)S(1)} collective-permute-done((f32[48,256]{1,0:T(8,128)S(1)}, f32[48,256]{1,0:T(8,128)S(1)}, u32[]{:S(2)}, u32[]{:S(2)}) %collective-permute-start.17) | collective-permute-done | bytes 49184 | tf_op jit(solution)/shard_map/ppermute | solution.py:13
  78.7 3.2 %collective-permute-start.18 = (f32[24,256]{1,0:T(8,128)S(1)}, f32[24,256]{1,0:T(8,128)S(1)}, u32[]{:S(2)}, u32[]{:S(2)}) collective-permute-start(f32[24,256]{1,0:T(8,128)S(1)} %slice.104), channel_id=1, source_target_pairs={{0,8},{1,9},{2,10},{3,11},{4,12},{5,13},{6,14},{7,15},{8,0},{9,1},... | collective-permute-start | bytes 73736 | tf_op jit(solution)/shard_map/ppermute | solution.py:13
  81.9 1.8 %collective-permute-done.18 = f32[24,256]{1,0:T(8,128)S(1)} collective-permute-done((f32[24,256]{1,0:T(8,128)S(1)}, f32[24,256]{1,0:T(8,128)S(1)}, u32[]{:S(2)}, u32[]{:S(2)}) %collective-permute-start.18) | collective-permute-done | bytes 24608 | tf_op jit(solution)/shard_map/ppermute | solution.py:13
  83.6 0.4 fusion.14
  84.0 0.1 slice_select_fusion
  84.1 1.2 %collective-permute-done.19 = f32[12,16]{0,1:T(8,128)S(1)} collective-permute-done((f32[12,16]{0,1:T(8,128)S(1)}, f32[12,16]{0,1:T(8,128)S(1)}, u32[]{:S(2)}, u32[]{:S(2)}) %collective-permute-start.19) | collective-permute-done | bytes 800 | tf_op jit(solution)/shard_map/ppermute | solution.py:13
  85.3 0.1 select_add_fusion
  85.4 0.7 copy.33
  (45 shorter events, 0.5 us)
Async XLA Ops:
  0.0 44.9 %copy-start = (bf16[1,4096,32]{1,2,0:T(8,128)(2,1)S(1)}, bf16[1,4096,32]{1,2,0:T(8,128)(2,1)}, u32[]{:S(2)}) copy-start(bf16[1,4096,32]{1,2,0:T(8,128)(2,1)} %param.10) | copy-start | bytes 786436
  0.0 35.5 %copy-start.1 = (bf16[1,14336,32]{1,2,0:T(8,128)(2,1)S(1)}, bf16[1,14336,32]{1,2,0:T(8,128)(2,1)}, u32[]{:S(2)}) copy-start(bf16[1,14336,32]{1,2,0:T(8,128)(2,1)} %param.11) | copy-start | bytes 2752516
  1.0 1.5 %collective-permute-start = (bf16[12,2048]{1,0:T(8,128)(2,1)S(1)}, bf16[12,2048]{1,0:T(8,128)(2,1)S(1)}, u32[]{:S(2)}, u32[]{:S(2)}) collective-permute-start(bf16[12,2048]{1,0:T(8,128)(2,1)S(1)} %get-tuple-element.11), channel_id=1, source_target_pairs={{0,1},{1,0},{2,3},{3,2},{4,5},{5,4},{6,7},{7,6},{8,9},{9,8},{10,11... | collective-permute-start | bytes 147464 | tf_op jit(solution)/shard_map/ppermute | solution.py:13
  2.4 5.9 %collective-permute-start.9 = (bf16[12,2048]{1,0:T(8,128)(2,1)S(1)}, bf16[12,2048]{1,0:T(8,128)(2,1)S(1)}, u32[]{:S(2)}, u32[]{:S(2)}) collective-permute-start(bf16[12,2048]{1,0:T(8,128)(2,1)S(1)} %get-tuple-element.13), channel_id=1, source_target_pairs={{0,1},{1,0},{2,3},{3,2},{4,5},{5,4},{6,7},{7,6},{8,9},{9,8},{10,11... | collective-permute-start | bytes 147464 | tf_op jit(solution)/shard_map/ppermute | solution.py:13
  2.6 10.2 %collective-permute-start.1 = (bf16[24,2048]{1,0:T(8,128)(2,1)S(1)}, bf16[24,2048]{1,0:T(8,128)(2,1)S(1)}, u32[]{:S(2)}, u32[]{:S(2)}) collective-permute-start(bf16[24,2048]{1,0:T(8,128)(2,1)S(1)} %get-tuple-element.6), channel_id=1, source_target_pairs={{0,8},{1,9},{2,10},{3,11},{4,12},{5,13},{6,14},{7,15},{8,0},{9,1},... | collective-permute-start | bytes 294920 | tf_op jit(solution)/shard_map/ppermute | solution.py:13
  6.7 12.3 %collective-permute-start.2 = (bf16[24,2048]{1,0:T(8,128)(2,1)S(1)}, bf16[24,2048]{1,0:T(8,128)(2,1)S(1)}, u32[]{:S(2)}, u32[]{:S(2)}) collective-permute-start(bf16[24,2048]{1,0:T(8,128)(2,1)S(1)} %get-tuple-element.6), channel_id=1, source_target_pairs={{0,4},{1,5},{2,6},{3,7},{4,0},{5,1},{6,2},{7,3},{8,12},{9,13},{10,... | collective-permute-start | bytes 294920 | tf_op jit(solution)/shard_map/ppermute | solution.py:13
  8.3 10.7 %collective-permute-start.3 = (bf16[24,2048]{1,0:T(8,128)(2,1)S(1)}, bf16[24,2048]{1,0:T(8,128)(2,1)S(1)}, u32[]{:S(2)}, u32[]{:S(2)}) collective-permute-start(bf16[24,2048]{1,0:T(8,128)(2,1)S(1)} %get-tuple-element.6), channel_id=1, source_target_pairs={{0,12},{1,13},{2,14},{3,15},{4,8},{5,9},{6,10},{7,11},{8,4},{9,5},... | collective-permute-start | bytes 294920 | tf_op jit(solution)/shard_map/ppermute | solution.py:13
  8.3 14.6 %collective-permute-start.10 = (bf16[24,2048]{1,0:T(8,128)(2,1)S(1)}, bf16[24,2048]{1,0:T(8,128)(2,1)S(1)}, u32[]{:S(2)}, u32[]{:S(2)}) collective-permute-start(bf16[24,2048]{1,0:T(8,128)(2,1)S(1)} %get-tuple-element.8), channel_id=1, source_target_pairs={{0,8},{1,9},{2,10},{3,11},{4,12},{5,13},{6,14},{7,15},{8,0},{9,1},... | collective-permute-start | bytes 294920 | tf_op jit(solution)/shard_map/ppermute | solution.py:13
  10.3 12.6 %collective-permute-start.11 = (bf16[24,2048]{1,0:T(8,128)(2,1)S(1)}, bf16[24,2048]{1,0:T(8,128)(2,1)S(1)}, u32[]{:S(2)}, u32[]{:S(2)}) collective-permute-start(bf16[24,2048]{1,0:T(8,128)(2,1)S(1)} %get-tuple-element.8), channel_id=1, source_target_pairs={{0,4},{1,5},{2,6},{3,7},{4,0},{5,1},{6,2},{7,3},{8,12},{9,13},{10,... | collective-permute-start | bytes 294920 | tf_op jit(solution)/shard_map/ppermute | solution.py:13
  12.8 10.2 %collective-permute-start.12 = (bf16[24,2048]{1,0:T(8,128)(2,1)S(1)}, bf16[24,2048]{1,0:T(8,128)(2,1)S(1)}, u32[]{:S(2)}, u32[]{:S(2)}) collective-permute-start(bf16[24,2048]{1,0:T(8,128)(2,1)S(1)} %get-tuple-element.8), channel_id=1, source_target_pairs={{0,12},{1,13},{2,14},{3,15},{4,8},{5,9},{6,10},{7,11},{8,4},{9,5},... | collective-permute-start | bytes 294920 | tf_op jit(solution)/shard_map/ppermute | solution.py:13
  19.0 10.8 %collective-permute-start.4 = (bf16[96,2048]{1,0:T(8,128)(2,1)S(1)}, bf16[96,2048]{1,0:T(8,128)(2,1)S(1)}, u32[]{:S(2)}, u32[]{:S(2)}) collective-permute-start(bf16[96,2048]{1,0:T(8,128)(2,1)S(1)} %pad_maximum_fusion), channel_id=1, source_target_pairs={{0,2},{1,3},{2,0},{3,1},{4,6},{5,7},{6,4},{7,5},{8,10},{9,11},{10,... | collective-permute-start | bytes 1179656 | tf_op jit(solution)/shard_map/ppermute | solution.py:13
  23.0 12.4 %collective-permute-start.13 = (bf16[96,2048]{1,0:T(8,128)(2,1)S(1)}, bf16[96,2048]{1,0:T(8,128)(2,1)S(1)}, u32[]{:S(2)}, u32[]{:S(2)}) collective-permute-start(bf16[96,2048]{1,0:T(8,128)(2,1)S(1)} %pad_maximum_fusion.1), channel_id=1, source_target_pairs={{0,2},{1,3},{2,0},{3,1},{4,6},{5,7},{6,4},{7,5},{8,10},{9,11},{10,... | collective-permute-start | bytes 1179656 | tf_op jit(solution)/shard_map/ppermute | solution.py:13
  29.8 15.1 %collective-permute-start.5 = (bf16[192,2048]{1,0:T(8,128)(2,1)S(1)}, bf16[192,2048]{1,0:T(8,128)(2,1)}, u32[]{:S(2)}, u32[]{:S(2)}) collective-permute-start(bf16[192,2048]{1,0:T(8,128)(2,1)S(1)} %constant_dynamic-update-slice_fusion), channel_id=1, source_target_pairs={{0,1},{1,0},{2,3},{3,2},{4,5},{5,4},{6,7},{7,6},{8,9},{9,8},{10,11... | collective-permute-start | bytes 2359304 | tf_op jit(solution)/shard_map/ppermute | solution.py:13
  35.4 13.5 %collective-permute-start.14 = (bf16[192,2048]{1,0:T(8,128)(2,1)S(1)}, bf16[192,2048]{1,0:T(8,128)(2,1)S(1)}, u32[]{:S(2)}, u32[]{:S(2)}) collective-permute-start(bf16[192,2048]{1,0:T(8,128)(2,1)S(1)} %constant_dynamic-update-slice_fusion.5), channel_id=1, source_target_pairs={{0,1},{1,0},{2,3},{3,2},{4,5},{5,4},{6,7},{7,6},{8,9},{9,8},{10,11... | collective-permute-start | bytes 2359304 | tf_op jit(solution)/shard_map/ppermute | solution.py:13
  36.7 29.2 %all-to-all-start = ((bf16[16,32,896]{2,1,0:T(8,128)(2,1)}), bf16[16,32,896]{2,1,0:T(8,128)(2,1)S(1)}, u32[]{:S(2)}, u32[]{:S(2)}) async-start(bf16[16,32,896]{2,1,0:T(8,128)(2,1)} %copy.32), calls=%async_computation | async-start | bytes 1835008 | tf_op jit(solution)/shard_map/all_to_all | solution.py:50
  47.0 9.1 %slice-start = ((s8[7340032]{0:T(1024)(128)(4,1)}), s8[4194304]{0:T(1024)(128)(4,1)S(1)}, s32[]{:S(2)}) async-start(s8[7340032]{0:T(1024)(128)(4,1)} %bitcast.26), calls=%async_computation.1 | async-start | bytes 8388608
  47.0 9.1 %slice-start.1 = ((s8[7340032]{0:T(1024)(128)(4,1)}), s8[3145728]{0:T(1024)(128)(4,1)S(1)}, s32[]{:S(2)}) async-start(s8[7340032]{0:T(1024)(128)(4,1)} %bitcast.26), calls=%async_computation.2 | async-start | bytes 6291456
  47.0 7.1 %collective-permute-start.6 = (f32[96,32]{0,1:T(8,128)S(1)}, f32[96,32]{0,1:T(8,128)S(1)}, u32[]{:S(2)}, u32[]{:S(2)}) collective-permute-start(f32[96,32]{0,1:T(8,128)S(1)} %get-tuple-element.18), channel_id=1, source_target_pairs={{0,2},{1,3},{2,0},{3,1},{4,6},{5,7},{6,4},{7,5},{8,10},{9,11},{10,... | collective-permute-start | bytes 36872 | tf_op jit(solution)/shard_map/ppermute | solution.py:13
  54.2 7.3 %collective-permute-start.7 = (f32[48,64]{0,1:T(8,128)S(1)}, f32[48,64]{0,1:T(8,128)S(1)}, u32[]{:S(2)}, u32[]{:S(2)}) collective-permute-start(f32[48,64]{0,1:T(8,128)S(1)} %get-tuple-element.16), channel_id=1, source_target_pairs={{0,4},{1,5},{2,6},{3,7},{4,0},{5,1},{6,2},{7,3},{8,12},{9,13},{10,... | collective-permute-start | bytes 36872 | tf_op jit(solution)/shard_map/ppermute | solution.py:13
  66.7 1.5 %collective-permute-start.15 = (f32[192,256]{1,0:T(8,128)S(1)}, f32[192,256]{1,0:T(8,128)S(1)}, u32[]{:S(2)}, u32[]{:S(2)}) collective-permute-start(f32[192,256]{1,0:T(8,128)S(1)} %convolution_add_fusion), channel_id=1, source_target_pairs={{0,1},{1,0},{2,3},{3,2},{4,5},{5,4},{6,7},{7,6},{8,9},{9,8},{10,11... | collective-permute-start | bytes 589832 | tf_op jit(solution)/shard_map/ppermute | solution.py:13
  68.5 5.0 %collective-permute-start.16 = (f32[96,256]{1,0:T(8,128)S(1)}, f32[96,256]{1,0:T(8,128)S(1)}, u32[]{:S(2)}, u32[]{:S(2)}) collective-permute-start(f32[96,256]{1,0:T(8,128)S(1)} %slice.100), channel_id=1, source_target_pairs={{0,2},{1,3},{2,0},{3,1},{4,6},{5,7},{6,4},{7,5},{8,10},{9,11},{10,... | collective-permute-start | bytes 294920 | tf_op jit(solution)/shard_map/ppermute | solution.py:13
  73.6 5.1 %collective-permute-start.17 = (f32[48,256]{1,0:T(8,128)S(1)}, f32[48,256]{1,0:T(8,128)S(1)}, u32[]{:S(2)}, u32[]{:S(2)}) collective-permute-start(f32[48,256]{1,0:T(8,128)S(1)} %slice.102), channel_id=1, source_target_pairs={{0,4},{1,5},{2,6},{3,7},{4,0},{5,1},{6,2},{7,3},{8,12},{9,13},{10,... | collective-permute-start | bytes 147464 | tf_op jit(solution)/shard_map/ppermute | solution.py:13
  76.6 5.3 %collective-permute-start.8 = (f32[24,128]{1,0:T(8,128)S(1)}, f32[24,128]{1,0:T(8,128)S(1)}, u32[]{:S(2)}, u32[]{:S(2)}) collective-permute-start(f32[24,128]{1,0:T(8,128)S(1)} %get-tuple-element.20), channel_id=1, source_target_pairs={{0,8},{1,9},{2,10},{3,11},{4,12},{5,13},{6,14},{7,15},{8,0},{9,1},... | collective-permute-start | bytes 36872 | tf_op jit(solution)/shard_map/ppermute | solution.py:13
  78.7 5.0 %collective-permute-start.18 = (f32[24,256]{1,0:T(8,128)S(1)}, f32[24,256]{1,0:T(8,128)S(1)}, u32[]{:S(2)}, u32[]{:S(2)}) collective-permute-start(f32[24,256]{1,0:T(8,128)S(1)} %slice.104), channel_id=1, source_target_pairs={{0,8},{1,9},{2,10},{3,11},{4,12},{5,13},{6,14},{7,15},{8,0},{9,1},... | collective-permute-start | bytes 73736 | tf_op jit(solution)/shard_map/ppermute | solution.py:13
  84.1 1.2 %collective-permute-start.19 = (f32[12,16]{0,1:T(8,128)S(1)}, f32[12,16]{0,1:T(8,128)S(1)}, u32[]{:S(2)}, u32[]{:S(2)}) collective-permute-start(f32[12,16]{0,1:T(8,128)S(1)} %slice_select_fusion), channel_id=1, source_target_pairs={{0,1},{1,0},{2,3},{3,2},{4,5},{5,4},{6,7},{7,6},{8,9},{9,8},{10,11... | collective-permute-start | bytes 2312 | tf_op jit(solution)/shard_map/ppermute | solution.py:13

commit v2 on v1

v2 whole, which is shorter than its diff:
```python
import functools

import jax
import jax.numpy as jnp
from jax import lax
from jax.experimental import pallas as pl
from jax.experimental.pallas import tpu as pltpu
from jax.sharding import PartitionSpec as P

AXIS = "query"
F32 = jnp.float32
BF16 = jnp.bfloat16
PAD = 16
LANES = 128


def swap(x, bit):
    n = lax.axis_size(AXIS)
    return lax.ppermute(x, AXIS, [(i, i ^ bit) for i in range(n)])


def pick(flag, when_zero, when_one):
    return jnp.where(flag == 0, when_zero, when_one)


def after(x, *others):
    return lax.optimization_barrier((x,) + others)[0]


def trade(x):
    return lax.all_to_all(x, AXIS, split_axis=0, concat_axis=0, tiled=True)


def nt_dot(a, b):
    return lax.dot_general(a, b, (((1,), (1,)), ((), ())), preferred_element_type=F32)


def z_order(planes):
    order = [0]
    bit = planes // 2
    while bit >= 1:
        order = order + [k | bit for k in order]
        bit //= 2
    return order


def row_offsets(n):
    return [(4 * k + 2 * y, c) for y in (0, 1) for k in z_order(n // 4) for c in (0, 1)]


def chip_rows(rows, core):
    half = rows.shape[1] // 2
    mine = pick(core, rows[:, :half], rows[:, half:])
    theirs = pick(core, rows[:, half:], rows[:, :half])
    other = swap(theirs, 1)
    return pick(core, jnp.concatenate([mine, other]), jnp.concatenate([other, mine]))


def group_rows(blocks, planes):
    column = jnp.concatenate([blocks[k] for k in z_order(planes)])
    both = jnp.concatenate([column, swap(column, 2)])
    return both, swap(both, 1)


def plain_hidden(core, own, other, gate_weight, up_weight):
    both = pick(core, jnp.concatenate([own, other], 1), jnp.concatenate([other, own], 1))
    gate = jnp.dot(both, gate_weight, preferred_element_type=F32)
    up = jnp.dot(both, up_weight, preferred_element_type=F32)
    hidden = jax.nn.silu(gate) * up
    head = lax.reduce_precision(hidden, exponent_bits=8, mantissa_bits=7)
    return head.astype(BF16), (hidden - head).astype(BF16)


class Layout:
    def __init__(self, n, cols, depth, rows, rank):
        self.n, self.cols, self.depth, self.rows, self.rank = n, cols, depth, rows, rank
        self.part = cols // LANES // 3 * LANES
        self.common = cols - 2 * self.part
        self.left = depth // 2
        self.wide = n // 2 * rank

    def fits(self, groups):
        return (
            groups % 2 == 0
            and self.cols % LANES == 0
            and self.part > 0
            and self.depth % (2 * LANES) == 0
            and self.depth // LANES * PAD <= self.rank
            and self.rows <= PAD
        )


def pack_kernel(lay, plane_ref, right_hbm, left_hbm, grad_hbm, split_ref, rest_ref, right_ref, left_ref, grad_ref, sems):
    copies = [
        pltpu.make_async_copy(source, to, sems.at[at])
        for at, (source, to) in enumerate(((right_hbm, right_ref), (left_hbm, left_ref), (grad_hbm, grad_ref)))
    ]
    for copy in copies:
        copy.start()
    for copy in copies:
        copy.wait()
    plane = plane_ref[0]
    cols, depth, part, common = lay.cols, lay.depth, lay.part, lay.common
    for to in range(lay.n):
        at = pl.multiple_of(to * cols + plane * part, LANES)
        split_ref[to, :, :part] = right_ref[:, pl.ds(at, part)]
        at = pl.multiple_of(to * depth + plane * lay.left, LANES)
        split_ref[to, :, part:] = left_ref[:, pl.ds(at, lay.left)]
        rest_ref[to, :, :common] = right_ref[:, to * cols + 2 * part : (to + 1) * cols]
        grad = grad_ref[:, to * depth : (to + 1) * depth].astype(F32)
        grad = jnp.concatenate([grad, jnp.zeros((PAD - lay.rows, depth), F32)]).astype(BF16)
        for piece in range(depth // LANES):
            rest_ref[to, piece * PAD : (piece + 1) * PAD, common:] = grad[:, piece * LANES : (piece + 1) * LANES]


def pack(lay, plane, right, left, grads):
    whole, away = pl.BlockSpec(memory_space=pltpu.VMEM), pl.BlockSpec(memory_space=pl.ANY)
    return pl.pallas_call(
        functools.partial(pack_kernel, lay),
        in_specs=[pl.BlockSpec(memory_space=pltpu.SMEM), away, away, away],
        out_specs=[whole, whole],
        out_shape=[
            jax.ShapeDtypeStruct((lay.n, lay.rank, lay.part + lay.left), BF16),
            jax.ShapeDtypeStruct((lay.n, lay.rank, lay.common + LANES), BF16),
        ],
        scratch_shapes=[pltpu.VMEM(x.shape, BF16) for x in (right, left, grads)] + [pltpu.SemaphoreType.DMA((3,))],
        compiler_params=pltpu.CompilerParams(vmem_limit_bytes=16 * 2**20),
        cost_estimate=pl.CostEstimate(flops=1000, bytes_accessed=1000, transcendentals=0),
        name="pack",
    )(plane.reshape(1), right, left, grads)


def hidden_kernel(steps, core_ref, own_ref, other_ref, gate_ref, up_ref, high_ref, low_ref, gate, up):
    step = pl.program_id(0)

    @pl.when(step == 0)
    def _():
        gate[...] = jnp.zeros_like(gate)
        up[...] = jnp.zeros_like(up)

    def add(rows_ref):
        rows = rows_ref[...]
        gate[...] += jnp.dot(rows, gate_ref[...], preferred_element_type=F32)
        up[...] += jnp.dot(rows, up_ref[...], preferred_element_type=F32)

    pl.when(step < steps)(lambda: add(own_ref))
    pl.when(step >= steps)(lambda: add(other_ref))

    @pl.when(step == 2 * steps - 1)
    def _():
        value = gate[...]
        hidden = value / (1.0 + jnp.exp(-value)) * up[...]
        high = hidden.astype(BF16)
        high_ref[...] = high
        low_ref[...] = (hidden - high.astype(F32)).astype(BF16)


def hidden_parts(core, own, other, gate_weight, up_weight):
    rows, half = own.shape
    cols = gate_weight.shape[1]
    steps = max(1, half // 512)
    step_rows = half // steps
    weight = pl.BlockSpec((step_rows, cols), lambda s, core_ref: ((core_ref[0] * steps + s) % (2 * steps), 0))
    out = pl.BlockSpec((rows, cols), lambda s, core_ref: (0, 0))
    return pl.pallas_call(
        functools.partial(hidden_kernel, steps),
        grid_spec=pltpu.PrefetchScalarGridSpec(
            num_scalar_prefetch=1,
            grid=(2 * steps,),
            in_specs=[
                pl.BlockSpec((rows, step_rows), lambda s, core_ref: (0, jnp.minimum(s, steps - 1))),
                pl.BlockSpec((rows, step_rows), lambda s, core_ref: (0, jnp.maximum(s - steps, 0))),
                weight,
                weight,
            ],
            out_specs=[out, out],
            scratch_shapes=[pltpu.VMEM((rows, cols), F32)] * 2,
        ),
        out_shape=[jax.ShapeDtypeStruct((rows, cols), BF16)] * 2,
        compiler_params=pltpu.CompilerParams(vmem_limit_bytes=48 * 2**20),
        cost_estimate=pl.CostEstimate(flops=1000, bytes_accessed=1000, transcendentals=0),
        name="hidden",
    )(core.reshape(1), own, other, gate_weight, up_weight)


def term_kernel(lay, at_ref, high_ref, low_ref, split_ref, twin_ref, rest_ref, keep_ref, send_ref, right, left, grad):
    here, plane = at_ref[0], at_ref[1]
    core = here & 1
    n, part, common, rank, rows, wide = lay.n, lay.part, lay.common, lay.rank, lay.rows, lay.wide
    for at, (offset, c) in enumerate(row_offsets(n)):
        source = ((here - core) ^ offset) + c
        for piece in range(lay.depth // LANES):
            grad[at * PAD : (at + 1) * PAD, piece * LANES : (piece + 1) * LANES] = rest_ref[
                source, piece * PAD : (piece + 1) * PAD, common:
            ]
    for turn, (out_ref, which) in enumerate(((send_ref, 1 - core), (keep_ref, core))):
        for pair in range(n // 2):
            query = 2 * pair + which
            block = slice(pair * rank, (pair + 1) * rank)
            halves = split_ref[query], twin_ref[query]
            for side in (0, 1):
                half = jnp.where(plane == side, halves[0], halves[1])
                right[turn, block, side * part : (side + 1) * part] = half[:, :part]
                left[turn, block, side * lay.left : (side + 1) * lay.left] = half[:, part:]
            right[turn, block, 2 * part :] = rest_ref[query, :, :common]
        out_ref[:, :wide] = nt_dot(high_ref[...], right[turn]) + nt_dot(low_ref[...], right[turn])
        padded = nt_dot(grad[...], left[turn])
        for at in range(n):
            out_ref[at * rows : (at + 1) * rows, wide:] = padded[at * PAD : at * PAD + rows]


def terms(lay, here, plane, high, low, split, twin, rest):
    whole = pl.BlockSpec(memory_space=pltpu.VMEM)
    return pl.pallas_call(
        functools.partial(term_kernel, lay),
        in_specs=[pl.BlockSpec(memory_space=pltpu.SMEM)] + [whole] * 5,
        out_specs=[whole, whole],
        out_shape=[jax.ShapeDtypeStruct((lay.n * lay.rows, 2 * lay.wide), F32)] * 2,
        scratch_shapes=[
            pltpu.VMEM((2, lay.wide, lay.cols), BF16),
            pltpu.VMEM((2, lay.wide, lay.depth), BF16),
            pltpu.VMEM((lay.n * PAD, lay.depth), BF16),
        ],
        compiler_params=pltpu.CompilerParams(vmem_limit_bytes=24 * 2**20),
        name="terms",
    )(jnp.stack([here, plane]), high, low, split, twin, rest)


def plain_terms(here, high, low, right, left, grads):
    n, rank = right.shape[:2]
    core = here & 1
    sources = [((here - core) ^ offset) + c for offset, c in row_offsets(n)]
    grads = jnp.concatenate([lax.dynamic_index_in_dim(grads, source, keepdims=False) for source in sources])
    outs = []
    for which in (core, 1 - core):
        some = lambda x: pick(which, *jnp.moveaxis(x.reshape(n // 2, 2, rank, -1), 1, 0)).reshape(n // 2 * rank, -1)
        some_right, some_left = some(right), some(left)
        outs.append(jnp.concatenate([nt_dot(high, some_right) + nt_dot(low, some_right), nt_dot(grads, some_left)], 1))
    return outs


def body(tokens, grad_out, gate_weight, up_weight, query_left, query_right):
    n = lax.axis_size(AXIS)
    planes = n // 4
    here = lax.axis_index(AXIS)
    core = here & 1
    own, width = tokens.shape
    rank = query_right.shape[2]
    cols = gate_weight.shape[1]
    depth = width // n
    right_own, left_own = query_right[0].T, query_left[0].T
    lay = Layout(n, cols, width // n, own, rank)
    fits = lay.fits(lax.axis_size("groups"))

    chip = chip_rows(tokens, core)
    blocks = {0: chip}
    for k in range(1, planes):
        blocks[k] = swap(chip, 4 * k)

    if fits:
        plane = lax.axis_index("groups") & 1
        split, rest = pack(lay, plane, right_own, left_own, grad_out)
        split = trade(after(split, blocks[1]))
        rest = trade(after(rest, *blocks.values()))
        groups = lax.axis_size("groups")
        twin = lax.ppermute(split, "groups", [(g, g ^ 1) for g in range(groups)])
    else:
        cut = lambda x: x.reshape(x.shape[0], n, -1).transpose(1, 0, 2)
        right_all, left_all, grad_all = (trade(cut(x)) for x in (right_own, left_own, grad_out))

    own_half, other_half = group_rows(blocks, planes)
    if fits:
        high, low = hidden_parts(core, own_half, other_half, gate_weight, up_weight)
        keep, send = terms(lay, here, plane, high, low, split, twin, rest)
    else:
        high, low = plain_hidden(core, own_half, other_half, gate_weight, up_weight)
        keep, send = plain_terms(here, high, low, right_all, left_all, grad_all)

    sums = keep + swap(send, 1)
    bit = 2
    while bit < n:
        half = sums.shape[0] // 2
        sums = sums[:half] + swap(sums[half:], bit)
        bit *= 2

    wide = n // 2 * rank
    spread = lax.broadcasted_iota(jnp.int32, (wide, n), 0) // rank * 2 + core
    spread = (spread == lax.broadcasted_iota(jnp.int32, (wide, n), 1)).astype(F32)
    scores = jnp.dot(sums[:, :wide] * sums[:, wide:], spread, precision=lax.Precision.HIGHEST)
    return pick(core, scores[:own], scores[own:]) + swap(pick(core, scores[own:], scores[:own]), 1)


def solution(mesh):
    return jax.shard_map(
        body,
        mesh=mesh,
        in_specs=(
            P(("groups", "query"), None),
            P(("groups", "query"), None),
            P(None, "query"),
            P(None, "query"),
            P("query", None, None),
            P("query", None, None),
        ),
        out_specs=P(("groups", "query"), None),
        check_vma=False,
    )
```

time: 86.3 us -> 72 us (0.83)
  starting transfers between devices: 41.8 us -> 24.7 us
  Pallas kernels: 0 us -> 12.7 us
  matrix products: 10.7 us -> 0.38 us
  local copies, waits for them, and re-layouts: 2.3 us -> 3.79 us
  other arithmetic: 2.38 us -> 1.31 us
    ppermute x20 -> x11, starting transfers between devices: 33.7 us -> 13.5 us  [swap(): return lax.ppermute(x, AXIS, [(i, i ^ bit) for i in range(n)])]
    pallas_call x0 -> x3, Pallas kernels: none -> 12.7 us  [the longest x1 9.85 us: hidden_parts(): pl.pallas_call(functools.partial(hidden_kernel, steps), grid_spec=pltpu.P...]
    dot_general x8 -> x1, matrix products: 10.7 us -> 0.38 us  [body(): jnp.dot(sums[:, :wide] * sums[:, wide:], spread, precision=lax.Precision....]
    ppermute x20 -> x11, waiting for transfers between devices: 24.2 us -> 16 us  [swap(): return lax.ppermute(x, AXIS, [(i, i ^ bit) for i in range(n)])]
    all_to_all x1 -> x2, waiting for transfers between devices: 4.41 us -> 12.3 us  [trade(): return lax.all_to_all(x, AXIS, split_axis=0, concat_axis=0, tiled=True)]
    unnamed x15 -> x9, local copies, waits for them, and re-layouts: 0.16 us -> 3.06 us
    all_to_all x1 -> x2, starting transfers between devices: 8.12 us -> 9.74 us  [trade(): return lax.all_to_all(x, AXIS, split_axis=0, concat_axis=0, tiled=True)]
    ppermute x0 -> x1, starting transfers between devices: none -> 1.49 us  [body(): twin = lax.ppermute(split, 'groups', [(g, g ^ 1) for g in range(groups)])]
  transfers between devices with their start and end apart: 21 -> 14, of which waited for: 10 -> 9; matrix products, arithmetic and copies ran while one was open for 14% -> 0% of each run, Pallas kernels for 0% -> 16%
where the time goes in v2:
time: 72 us; the launch traced here: 71.4 us
  waiting for transfers between devices  28.3 us (39%)
  starting transfers between devices  24.7 us (34%)
  Pallas kernels  12.7 us (18%)
  local copies, waits for them, and re-layouts  3.79 us (5%)
  other arithmetic  1.31 us (2%)
    ppermute x11, waiting for transfers between devices, swap(): return lax.ppermute(x, AXIS, [(i, i ^ bit) for i in range(n)])  16 us
    ppermute x11, starting transfers between devices, swap(): return lax.ppermute(x, AXIS, [(i, i ^ bit) for i in range(n)])  13.5 us
    all_to_all x2, waiting for transfers between devices, trade(): return lax.all_to_all(x, AXIS, split_axis=0, concat_axis=0, tiled=True)  12.3 us
    pallas_call x1, Pallas kernels, hidden_parts(): pl.pallas_call(functools.partial(hidden_kernel, steps), grid_spec=pltpu.P...  9.85 us
    all_to_all x2, starting transfers between devices, trade(): return lax.all_to_all(x, AXIS, split_axis=0, concat_axis=0, tiled=True)  9.74 us
    unnamed x9, local copies, waits for them, and re-layouts  3.06 us
    ppermute x1, starting transfers between devices, body(): twin = lax.ppermute(split, 'groups', [(g, g ^ 1) for g in range(groups)])  1.49 us
    pallas_call x1, Pallas kernels, pack(): pl.pallas_call(functools.partial(pack_kernel, lay), in_specs=[pl.BlockSpe...  1.49 us
  transfers between devices with their start and end apart: 14, of which 9 were waited for; matrix products, arithmetic and copies ran while one was open for 0% of the time, Pallas kernels for 16%

profile of v2, /device:TPU:0, one launch (start us, length us, event | category | flops | bytes accessed | tf_op | source)
XLA Modules:
  0.0 71.4 jit_solution(226694746829888465)
XLA Ops:
  0.0 0.9 %broadcast_select_fusion = (bf16[12,2048]{1,0:T(8,128)(2,1)S(1)}, bf16[12,2048]{1,0:T(8,128)(2,1)S(1)}) fusion(pred[]{:T(512)S(6)} %eq.4, bf16[12,4096]{1,0:T(8,128)(2,1)} %param.6), kind=kLoop, calls=%fused_computation.11 | loop fusion | flops 49152 | bytes 196609 | tf_op jit(solution)/shard_map/jit(_where)/select_n | solution.py:23
  0.9 0.5 collective-permute-start
  1.4 0.9 %collective-permute-done = bf16[12,2048]{1,0:T(8,128)(2,1)S(1)} collective-permute-done((bf16[12,2048]{1,0:T(8,128)(2,1)S(1)}, bf16[12,2048]{1,0:T(8,128)(2,1)S(1)}, u32[]{:S(2)}, u32[]{:S(2)}) %collective-permute-start) | collective-permute-done | bytes 49184 | tf_op jit(solution)/shard_map/ppermute | solution.py:19
  2.3 0.1 constant_dynamic-update-slice_fusion.4
  2.4 3.0 %collective-permute-start.2 = (bf16[24,2048]{1,0:T(8,128)(2,1)S(1)}, bf16[24,2048]{1,0:T(8,128)(2,1)S(1)}, u32[]{:S(2)}, u32[]{:S(2)}) collective-permute-start(bf16[24,2048]{1,0:T(8,128)(2,1)S(1)} %get-tuple-element.22), channel_id=1, source_target_pairs={{0,4},{1,5},{2,6},{3,7},{4,0},{5,1},{6,2},{7,3},{8,12},{9,13},{10,... | collective-permute-start | bytes 294920 | tf_op jit(solution)/shard_map/ppermute | solution.py:19
  5.4 2.6 %collective-permute-start.1 = (bf16[24,2048]{1,0:T(8,128)(2,1)S(1)}, bf16[24,2048]{1,0:T(8,128)(2,1)S(1)}, u32[]{:S(2)}, u32[]{:S(2)}) collective-permute-start(bf16[24,2048]{1,0:T(8,128)(2,1)S(1)} %get-tuple-element.22), channel_id=1, source_target_pairs={{0,8},{1,9},{2,10},{3,11},{4,12},{5,13},{6,14},{7,15},{8,0},{9,1},... | collective-permute-start | bytes 294920 | tf_op jit(solution)/shard_map/ppermute | solution.py:19
  7.9 0.0 collective-permute-start.3
  7.9 0.0 copy-start
  7.9 1.2 %copy-done = bf16[1,14336,32]{1,2,0:T(8,128)(2,1)S(1)} copy-done((bf16[1,14336,32]{1,2,0:T(8,128)(2,1)S(1)}, bf16[1,14336,32]{1,2,0:T(8,128)(2,1)}, u32[]{:S(2)}) %copy-start) | copy-done | bytes 917528
  9.1 0.0 copy-start.1
  9.1 0.9 %copy-done.1 = bf16[1,4096,32]{1,2,0:T(8,128)(2,1)S(1)} copy-done((bf16[1,4096,32]{1,2,0:T(8,128)(2,1)S(1)}, bf16[1,4096,32]{1,2,0:T(8,128)(2,1)}, u32[]{:S(2)}) %copy-start.1) | copy-done | bytes 262168
  10.1 0.0 copy-start.2
  10.1 0.9 %copy-done.2 = bf16[12,4096]{1,0:T(8,128)(2,1)S(1)} copy-done((bf16[12,4096]{1,0:T(8,128)(2,1)S(1)}, bf16[12,4096]{1,0:T(8,128)(2,1)}, u32[]{:S(2)}) %copy-start.2) | copy-done | bytes 98328
  11.0 1.5 %pack.1 = (bf16[16,32,384]{2,1,0:T(8,128)(2,1)}, bf16[16,32,512]{2,1,0:T(8,128)(2,1)}) custom-call(s32[1]{0:T(128)} %bitcast.1.plane_ref, bf16[32,14336]{1,0:T(8,128)(2,1)S(1)} %bitcast.9, bf16[32,4096]{1,0:T(8,128)(2,1)S(1)} %bitcast.10, bf16[12,4096]{1,0:T(8,128)(2,1)S(1)} %copy-done.2), custom_call_target="tpu_custom_call" | custom-call | flops 1000 | bytes 1000 | tf_op jit(solution)/shard_map/pack/pallas_call | solution.py:118
  12.5 0.0 collective-permute-done.2
  12.5 6.2 %all-to-all-start = ((bf16[16,32,384]{2,1,0:T(8,128)(2,1)}), bf16[16,32,384]{2,1,0:T(8,128)(2,1)S(1)}, u32[]{:S(2)}, u32[]{:S(2)}) async-start(bf16[16,32,384]{2,1,0:T(8,128)(2,1)} %get-tuple-element.16), calls=%async_computation | async-start | bytes 786432 | tf_op jit(solution)/shard_map/all_to_all | solution.py:31
  18.7 0.0 collective-permute-done.1
  18.7 0.0 collective-permute-done.3
  18.7 2.0 %collective-permute-start.4 = (bf16[96,2048]{1,0:T(8,128)(2,1)S(1)}, bf16[96,2048]{1,0:T(8,128)(2,1)S(1)}, u32[]{:S(2)}, u32[]{:S(2)}) collective-permute-start(bf16[96,2048]{1,0:T(8,128)(2,1)S(1)} %pad_maximum_fusion), channel_id=1, source_target_pairs={{0,2},{1,3},{2,0},{3,1},{4,6},{5,7},{6,4},{7,5},{8,10},{9,11},{10,... | collective-permute-start | bytes 1179656 | tf_op jit(solution)/shard_map/ppermute | solution.py:19
  20.7 10.1 %all-to-all-done.split_ref = bf16[16,32,384]{2,1,0:T(8,128)(2,1)S(1)} async-done(((bf16[16,32,384]{2,1,0:T(8,128)(2,1)}), bf16[16,32,384]{2,1,0:T(8,128)(2,1)S(1)}, u32[]{:S(2)}, u32[]{:S(2)}) %all-to-all-start) | async-done | bytes 393248 | tf_op jit(solution)/shard_map/all_to_all | solution.py:31
  30.9 3.6 %all-to-all-start.1 = ((bf16[16,32,512]{2,1,0:T(8,128)(2,1)}), bf16[16,32,512]{2,1,0:T(8,128)(2,1)S(1)}, u32[]{:S(2)}, u32[]{:S(2)}) async-start(bf16[16,32,512]{2,1,0:T(8,128)(2,1)} %get-tuple-element.18), calls=%async_computation.1 | async-start | bytes 1048576 | tf_op jit(solution)/shard_map/all_to_all | solution.py:31
  34.5 0.0 collective-permute-done.4
  34.5 0.4 collective-permute-start.5
  34.9 1.5 %collective-permute-start.6 = (bf16[16,32,384]{2,1,0:T(8,128)(2,1)S(1)}, bf16[16,32,384]{2,1,0:T(8,128)(2,1)S(1)}, u32[]{:S(2)}, u32[]{:S(2)}) collective-permute-start(bf16[16,32,384]{2,1,0:T(8,128)(2,1)S(1)} %all-to-all-done.split_ref), channel_id=1, source_target_pairs={{0,16},{16,0},{1,17},{17,1},{2,18},{18,2},{3,19},{19,3},{4,20},{20... | collective-permute-start | bytes 1179656 | tf_op jit(solution)/shard_map/ppermute | solution.py:266
  36.4 0.1 pad_add_fusion.at_ref
  36.5 0.4 collective-permute-done.5.other_ref
  36.9 9.9 %hidden.1 = (bf16[192,896]{1,0:T(8,128)(2,1)S(1)}, bf16[192,896]{1,0:T(8,128)(2,1)S(1)}) custom-call(s32[1]{0:T(128)} %bitcast.2.core_ref, bf16[192,2048]{1,0:T(8,128)(2,1)S(1)} %constant_dynamic-update-slice_fusion.own_ref, bf16[192,2048]{1,0:T(8,128)(2,1)S(1)} %collective-permute-done.5.other_ref, bf16[4096,896]{1,0:T(8,128)(2,1)} %gate_ref.1, ...), custom_call_target="tpu_custom_call" | custom-call | flops 1000 | bytes 1000 | tf_op jit(solution)/shard_map/hidden/pallas_call | solution.py:165
  46.7 2.2 %all-to-all-done.1.rest_ref = bf16[16,32,512]{2,1,0:T(8,128)(2,1)S(1)} async-done(((bf16[16,32,512]{2,1,0:T(8,128)(2,1)}), bf16[16,32,512]{2,1,0:T(8,128)(2,1)S(1)}, u32[]{:S(2)}, u32[]{:S(2)}) %all-to-all-start.1) | async-done | bytes 524320 | tf_op jit(solution)/shard_map/all_to_all | solution.py:31
  48.9 0.0 collective-permute-done.6.twin_ref
  48.9 1.4 %terms.1 = (f32[192,512]{1,0:T(8,128)S(1)}, f32[192,512]{1,0:T(8,128)S(1)}) custom-call(s32[2]{0:T(128)S(1)} %pad_add_fusion.at_ref, bf16[192,896]{1,0:T(8,128)(2,1)S(1)} %get-tuple-element.13.high_ref, bf16[192,896]{1,0:T(8,128)(2,1)S(1)} %get-tuple-element.14.low_ref, bf16[16,32,384]{2,1,0:T(8,128)(2,1)S(1)} %all-to-all-done.split_ref, ...), custom_call_target="tpu_custom_call" | custom-call | tf_op jit(solution)/shard_map/terms/pallas_call | solution.py:214
  50.3 0.1 collective-permute-start.7
  50.4 1.7 %collective-permute-done.7 = f32[192,512]{1,0:T(8,128)S(1)} collective-permute-done((f32[192,512]{1,0:T(8,128)S(1)}, f32[192,512]{1,0:T(8,128)S(1)}, u32[]{:S(2)}, u32[]{:S(2)}) %collective-permute-start.7) | collective-permute-done | bytes 393248 | tf_op jit(solution)/shard_map/ppermute | solution.py:19
  52.1 0.1 add.23
  52.2 0.9 %collective-permute-start.8 = (f32[96,512]{1,0:T(8,128)S(1)}, f32[96,512]{1,0:T(8,128)S(1)}, u32[]{:S(2)}, u32[]{:S(2)}) collective-permute-start(f32[96,512]{1,0:T(8,128)S(1)} %slice.53), channel_id=1, source_target_pairs={{0,2},{1,3},{2,0},{3,1},{4,6},{5,7},{6,4},{7,5},{8,10},{9,11},{10,... | collective-permute-start | bytes 589832 | tf_op jit(solution)/shard_map/ppermute | solution.py:19
  53.1 6.1 %collective-permute-done.8 = f32[96,512]{1,0:T(8,128)S(1)} collective-permute-done((f32[96,512]{1,0:T(8,128)S(1)}, f32[96,512]{1,0:T(8,128)S(1)}, u32[]{:S(2)}, u32[]{:S(2)}) %collective-permute-start.8) | collective-permute-done | bytes 196640 | tf_op jit(solution)/shard_map/ppermute | solution.py:19
  59.2 1.7 %collective-permute-start.9 = (f32[48,512]{1,0:T(8,128)S(1)}, f32[48,512]{1,0:T(8,128)S(1)}, u32[]{:S(2)}, u32[]{:S(2)}) collective-permute-start(f32[48,512]{1,0:T(8,128)S(1)} %slice.55), channel_id=1, source_target_pairs={{0,4},{1,5},{2,6},{3,7},{4,0},{5,1},{6,2},{7,3},{8,12},{9,13},{10,... | collective-permute-start | bytes 294920 | tf_op jit(solution)/shard_map/ppermute | solution.py:19
  60.9 3.0 %collective-permute-done.9 = f32[48,512]{1,0:T(8,128)S(1)} collective-permute-done((f32[48,512]{1,0:T(8,128)S(1)}, f32[48,512]{1,0:T(8,128)S(1)}, u32[]{:S(2)}, u32[]{:S(2)}) %collective-permute-start.9) | collective-permute-done | bytes 98336 | tf_op jit(solution)/shard_map/ppermute | solution.py:19
  64.0 2.3 %collective-permute-start.10 = (f32[24,512]{1,0:T(8,128)S(1)}, f32[24,512]{1,0:T(8,128)S(1)}, u32[]{:S(2)}, u32[]{:S(2)}) collective-permute-start(f32[24,512]{1,0:T(8,128)S(1)} %slice.57), channel_id=1, source_target_pairs={{0,8},{1,9},{2,10},{3,11},{4,12},{5,13},{6,14},{7,15},{8,0},{9,1},... | collective-permute-start | bytes 147464 | tf_op jit(solution)/shard_map/ppermute | solution.py:19
  66.3 2.7 %collective-permute-done.10 = f32[24,512]{1,0:T(8,128)S(1)} collective-permute-done((f32[24,512]{1,0:T(8,128)S(1)}, f32[24,512]{1,0:T(8,128)S(1)}, u32[]{:S(2)}, u32[]{:S(2)}) %collective-permute-start.10) | collective-permute-done | bytes 49184 | tf_op jit(solution)/shard_map/ppermute | solution.py:19
  69.0 0.4 fusion
  69.4 0.1 slice_select_fusion
  69.5 0.0 collective-permute-start.11
  69.5 1.2 %collective-permute-done.11 = f32[12,16]{0,1:T(8,128)S(1)} collective-permute-done((f32[12,16]{0,1:T(8,128)S(1)}, f32[12,16]{0,1:T(8,128)S(1)}, u32[]{:S(2)}, u32[]{:S(2)}) %collective-permute-start.11) | collective-permute-done | bytes 800 | tf_op jit(solution)/shard_map/ppermute | solution.py:19
  70.7 0.1 select_add_fusion
  70.7 0.7 copy.7
  (13 shorter events, 0.2 us)
Async XLA Ops:
  0.9 1.4 %collective-permute-start = (bf16[12,2048]{1,0:T(8,128)(2,1)S(1)}, bf16[12,2048]{1,0:T(8,128)(2,1)S(1)}, u32[]{:S(2)}, u32[]{:S(2)}) collective-permute-start(bf16[12,2048]{1,0:T(8,128)(2,1)S(1)} %get-tuple-element.23), channel_id=1, source_target_pairs={{0,1},{1,0},{2,3},{3,2},{4,5},{5,4},{6,7},{7,6},{8,9},{9,8},{10,11... | collective-permute-start | bytes 147464 | tf_op jit(solution)/shard_map/ppermute | solution.py:19
  2.4 10.1 %collective-permute-start.2 = (bf16[24,2048]{1,0:T(8,128)(2,1)S(1)}, bf16[24,2048]{1,0:T(8,128)(2,1)S(1)}, u32[]{:S(2)}, u32[]{:S(2)}) collective-permute-start(bf16[24,2048]{1,0:T(8,128)(2,1)S(1)} %get-tuple-element.22), channel_id=1, source_target_pairs={{0,4},{1,5},{2,6},{3,7},{4,0},{5,1},{6,2},{7,3},{8,12},{9,13},{10,... | collective-permute-start | bytes 294920 | tf_op jit(solution)/shard_map/ppermute | solution.py:19
  5.4 13.3 %collective-permute-start.1 = (bf16[24,2048]{1,0:T(8,128)(2,1)S(1)}, bf16[24,2048]{1,0:T(8,128)(2,1)S(1)}, u32[]{:S(2)}, u32[]{:S(2)}) collective-permute-start(bf16[24,2048]{1,0:T(8,128)(2,1)S(1)} %get-tuple-element.22), channel_id=1, source_target_pairs={{0,8},{1,9},{2,10},{3,11},{4,12},{5,13},{6,14},{7,15},{8,0},{9,1},... | collective-permute-start | bytes 294920 | tf_op jit(solution)/shard_map/ppermute | solution.py:19
  7.9 10.7 %collective-permute-start.3 = (bf16[24,2048]{1,0:T(8,128)(2,1)S(1)}, bf16[24,2048]{1,0:T(8,128)(2,1)S(1)}, u32[]{:S(2)}, u32[]{:S(2)}) collective-permute-start(bf16[24,2048]{1,0:T(8,128)(2,1)S(1)} %get-tuple-element.22), channel_id=1, source_target_pairs={{0,12},{1,13},{2,14},{3,15},{4,8},{5,9},{6,10},{7,11},{8,4},{9,5},... | collective-permute-start | bytes 294920 | tf_op jit(solution)/shard_map/ppermute | solution.py:19
  7.9 1.2 %copy-start = (bf16[1,14336,32]{1,2,0:T(8,128)(2,1)S(1)}, bf16[1,14336,32]{1,2,0:T(8,128)(2,1)}, u32[]{:S(2)}) copy-start(bf16[1,14336,32]{1,2,0:T(8,128)(2,1)} %param.11) | copy-start | bytes 2752516
  9.1 0.9 %copy-start.1 = (bf16[1,4096,32]{1,2,0:T(8,128)(2,1)S(1)}, bf16[1,4096,32]{1,2,0:T(8,128)(2,1)}, u32[]{:S(2)}) copy-start(bf16[1,4096,32]{1,2,0:T(8,128)(2,1)} %param.10) | copy-start | bytes 786436
  10.1 0.9 %copy-start.2 = (bf16[12,4096]{1,0:T(8,128)(2,1)S(1)}, bf16[12,4096]{1,0:T(8,128)(2,1)}, u32[]{:S(2)}) copy-start(bf16[12,4096]{1,0:T(8,128)(2,1)} %grad_hbm.1) | copy-start | bytes 294916
  12.5 18.4 %all-to-all-start = ((bf16[16,32,384]{2,1,0:T(8,128)(2,1)}), bf16[16,32,384]{2,1,0:T(8,128)(2,1)S(1)}, u32[]{:S(2)}, u32[]{:S(2)}) async-start(bf16[16,32,384]{2,1,0:T(8,128)(2,1)} %get-tuple-element.16), calls=%async_computation | async-start | bytes 786432 | tf_op jit(solution)/shard_map/all_to_all | solution.py:31
  18.7 15.8 %collective-permute-start.4 = (bf16[96,2048]{1,0:T(8,128)(2,1)S(1)}, bf16[96,2048]{1,0:T(8,128)(2,1)S(1)}, u32[]{:S(2)}, u32[]{:S(2)}) collective-permute-start(bf16[96,2048]{1,0:T(8,128)(2,1)S(1)} %pad_maximum_fusion), channel_id=1, source_target_pairs={{0,2},{1,3},{2,0},{3,1},{4,6},{5,7},{6,4},{7,5},{8,10},{9,11},{10,... | collective-permute-start | bytes 1179656 | tf_op jit(solution)/shard_map/ppermute | solution.py:19
  30.9 18.0 %all-to-all-start.1 = ((bf16[16,32,512]{2,1,0:T(8,128)(2,1)}), bf16[16,32,512]{2,1,0:T(8,128)(2,1)S(1)}, u32[]{:S(2)}, u32[]{:S(2)}) async-start(bf16[16,32,512]{2,1,0:T(8,128)(2,1)} %get-tuple-element.18), calls=%async_computation.1 | async-start | bytes 1048576 | tf_op jit(solution)/shard_map/all_to_all | solution.py:31
  34.5 2.4 %collective-permute-start.5 = (bf16[192,2048]{1,0:T(8,128)(2,1)S(1)}, bf16[192,2048]{1,0:T(8,128)(2,1)S(1)}, u32[]{:S(2)}, u32[]{:S(2)}) collective-permute-start(bf16[192,2048]{1,0:T(8,128)(2,1)S(1)} %constant_dynamic-update-slice_fusion.own_ref), channel_id=1, source_target_pairs={{0,1},{1,0},{2,3},{3,2},{4,5},{5,4},{6,7},{7,6},{8,9},{9,8},{10,11... | collective-permute-start | bytes 2359304 | tf_op jit(solution)/shard_map/ppermute | solution.py:19
  34.9 14.0 %collective-permute-start.6 = (bf16[16,32,384]{2,1,0:T(8,128)(2,1)S(1)}, bf16[16,32,384]{2,1,0:T(8,128)(2,1)S(1)}, u32[]{:S(2)}, u32[]{:S(2)}) collective-permute-start(bf16[16,32,384]{2,1,0:T(8,128)(2,1)S(1)} %all-to-all-done.split_ref), channel_id=1, source_target_pairs={{0,16},{16,0},{1,17},{17,1},{2,18},{18,2},{3,19},{19,3},{4,20},{20... | collective-permute-start | bytes 1179656 | tf_op jit(solution)/shard_map/ppermute | solution.py:266
  50.3 1.8 %collective-permute-start.7 = (f32[192,512]{1,0:T(8,128)S(1)}, f32[192,512]{1,0:T(8,128)S(1)}, u32[]{:S(2)}, u32[]{:S(2)}) collective-permute-start(f32[192,512]{1,0:T(8,128)S(1)} %get-tuple-element.20), channel_id=1, source_target_pairs={{0,1},{1,0},{2,3},{3,2},{4,5},{5,4},{6,7},{7,6},{8,9},{9,8},{10,11... | collective-permute-start | bytes 1179656 | tf_op jit(solution)/shard_map/ppermute | solution.py:19
  52.2 7.0 %collective-permute-start.8 = (f32[96,512]{1,0:T(8,128)S(1)}, f32[96,512]{1,0:T(8,128)S(1)}, u32[]{:S(2)}, u32[]{:S(2)}) collective-permute-start(f32[96,512]{1,0:T(8,128)S(1)} %slice.53), channel_id=1, source_target_pairs={{0,2},{1,3},{2,0},{3,1},{4,6},{5,7},{6,4},{7,5},{8,10},{9,11},{10,... | collective-permute-start | bytes 589832 | tf_op jit(solution)/shard_map/ppermute | solution.py:19
  59.2 4.7 %collective-permute-start.9 = (f32[48,512]{1,0:T(8,128)S(1)}, f32[48,512]{1,0:T(8,128)S(1)}, u32[]{:S(2)}, u32[]{:S(2)}) collective-permute-start(f32[48,512]{1,0:T(8,128)S(1)} %slice.55), channel_id=1, source_target_pairs={{0,4},{1,5},{2,6},{3,7},{4,0},{5,1},{6,2},{7,3},{8,12},{9,13},{10,... | collective-permute-start | bytes 294920 | tf_op jit(solution)/shard_map/ppermute | solution.py:19
  64.0 5.1 %collective-permute-start.10 = (f32[24,512]{1,0:T(8,128)S(1)}, f32[24,512]{1,0:T(8,128)S(1)}, u32[]{:S(2)}, u32[]{:S(2)}) collective-permute-start(f32[24,512]{1,0:T(8,128)S(1)} %slice.57), channel_id=1, source_target_pairs={{0,8},{1,9},{2,10},{3,11},{4,12},{5,13},{6,14},{7,15},{8,0},{9,1},... | collective-permute-start | bytes 147464 | tf_op jit(solution)/shard_map/ppermute | solution.py:19
  69.5 1.2 %collective-permute-start.11 = (f32[12,16]{0,1:T(8,128)S(1)}, f32[12,16]{0,1:T(8,128)S(1)}, u32[]{:S(2)}, u32[]{:S(2)}) collective-permute-start(f32[12,16]{0,1:T(8,128)S(1)} %slice_select_fusion), channel_id=1, source_target_pairs={{0,1},{1,0},{2,3},{3,2},{4,5},{5,4},{6,7},{7,6},{8,9},{9,8},{10,11... | collective-permute-start | bytes 2312 | tf_op jit(solution)/shard_map/ppermute | solution.py:19

commit v3 on v2

--- a/solution.py
+++ b/solution.py
@@ -48,11 +48,11 @@
     return [(4 * k + 2 * y, c) for y in (0, 1) for k in z_order(n // 4) for c in (0, 1)]
 
 
-def chip_rows(rows, core):
+def chip_rows(rows, core, also):
     half = rows.shape[1] // 2
     mine = pick(core, rows[:, :half], rows[:, half:])
     theirs = pick(core, rows[:, half:], rows[:, :half])
-    other = swap(theirs, 1)
+    other = after(swap(theirs, 1), *also)
     return pick(core, jnp.concatenate([mine, other]), jnp.concatenate([other, mine]))
 
 
@@ -77,7 +77,7 @@
         self.part = cols // LANES // 3 * LANES
         self.common = cols - 2 * self.part
         self.left = depth // 2
-        self.wide = n // 2 * rank
+        self.wide = n * rank
 
     def fits(self, groups):
         return (
@@ -87,6 +87,7 @@
             and self.depth % (2 * LANES) == 0
             and self.depth // LANES * PAD <= self.rank
             and self.rows <= PAD
+            and self.n % 16 == 0
         )
 
 
@@ -124,7 +125,7 @@
             jax.ShapeDtypeStruct((lay.n, lay.rank, lay.common + LANES), BF16),
         ],
         scratch_shapes=[pltpu.VMEM(x.shape, BF16) for x in (right, left, grads)] + [pltpu.SemaphoreType.DMA((3,))],
-        compiler_params=pltpu.CompilerParams(vmem_limit_bytes=16 * 2**20),
+        compiler_params=pltpu.CompilerParams(vmem_limit_bytes=56 * 2**20),
         cost_estimate=pl.CostEstimate(flops=1000, bytes_accessed=1000, transcendentals=0),
         name="pack",
     )(plane.reshape(1), right, left, grads)
@@ -183,7 +184,8 @@
     )(core.reshape(1), own, other, gate_weight, up_weight)
 
 
-def term_kernel(lay, at_ref, high_ref, low_ref, split_ref, twin_ref, rest_ref, keep_ref, send_ref, right, left, grad):
+def term_kernel(lay, at_ref, high_ref, low_ref, split_ref, twin_ref, rest_ref, *more):
+    keep_ref, send_ref, keep_left_ref, send_left_ref, right, left, grad = more
     here, plane = at_ref[0], at_ref[1]
     core = here & 1
     n, part, common, rank, rows, wide = lay.n, lay.part, lay.common, lay.rank, lay.rows, lay.wide
@@ -193,20 +195,29 @@
             grad[at * PAD : (at + 1) * PAD, piece * LANES : (piece + 1) * LANES] = rest_ref[
                 source, piece * PAD : (piece + 1) * PAD, common:
             ]
-    for turn, (out_ref, which) in enumerate(((send_ref, 1 - core), (keep_ref, core))):
+    for turn in (0, 1):
+        for at in range(n // 2):
+            query = turn * (n // 2) + at
+            block = slice(query * rank, (query + 1) * rank)
+            for side in (0, 1):
+                half = jnp.where(plane == side, split_ref[query], twin_ref[query])
+                right[block, side * part : (side + 1) * part] = half[:, :part]
+                left[block, side * lay.left : (side + 1) * lay.left] = half[:, part:]
+            right[block, 2 * part :] = rest_ref[query, :, :common]
+        block = slice(turn * wide // 2, (turn + 1) * wide // 2)
+        rights = nt_dot(high_ref[...], right[block]) + nt_dot(low_ref[...], right[block])
+        lefts = nt_dot(grad[...], left[block])
         for pair in range(n // 2):
-            query = 2 * pair + which
-            block = slice(pair * rank, (pair + 1) * rank)
-            halves = split_ref[query], twin_ref[query]
-            for side in (0, 1):
-                half = jnp.where(plane == side, halves[0], halves[1])
-                right[turn, block, side * part : (side + 1) * part] = half[:, :part]
-                left[turn, block, side * lay.left : (side + 1) * lay.left] = half[:, part:]
-            right[turn, block, 2 * part :] = rest_ref[query, :, :common]
-        out_ref[:, :wide] = nt_dot(high_ref[...], right[turn]) + nt_dot(low_ref[...], right[turn])
-        padded = nt_dot(grad[...], left[turn])
-        for at in range(n):
-            out_ref[at * rows : (at + 1) * rows, wide:] = padded[at * PAD : at * PAD + rows]
+            to = slice(pair * rows, (pair + 1) * rows)
+            first, second = rights[2 * pair * rows :][:rows], rights[(2 * pair + 1) * rows :][:rows]
+            keep_ref[to, block] = jnp.where(core == 0, first, second)
+            send_ref[to, block] = jnp.where(core == 0, second, first)
+            quarter = n // 8
+            at = (pair // quarter & 1) * 2 * quarter + (pair // quarter >> 1) * quarter + pair % quarter
+            to = slice(at * rows, (at + 1) * rows)
+            first, second = lefts[2 * pair * PAD :][:rows], lefts[(2 * pair + 1) * PAD :][:rows]
+            keep_left_ref[to, block] = jnp.where(core == 0, first, second)
+            send_left_ref[to, block] = jnp.where(core == 0, second, first)
 
 
 def terms(lay, here, plane, high, low, split, twin, rest):
@@ -214,11 +225,11 @@
     return pl.pallas_call(
         functools.partial(term_kernel, lay),
         in_specs=[pl.BlockSpec(memory_space=pltpu.SMEM)] + [whole] * 5,
-        out_specs=[whole, whole],
-        out_shape=[jax.ShapeDtypeStruct((lay.n * lay.rows, 2 * lay.wide), F32)] * 2,
+        out_specs=[whole] * 4,
+        out_shape=[jax.ShapeDtypeStruct((lay.n // 2 * lay.rows, lay.wide), F32)] * 4,
         scratch_shapes=[
-            pltpu.VMEM((2, lay.wide, lay.cols), BF16),
-            pltpu.VMEM((2, lay.wide, lay.depth), BF16),
+            pltpu.VMEM((lay.wide, lay.cols), BF16),
+            pltpu.VMEM((lay.wide, lay.depth), BF16),
             pltpu.VMEM((lay.n * PAD, lay.depth), BF16),
         ],
         compiler_params=pltpu.CompilerParams(vmem_limit_bytes=24 * 2**20),
@@ -228,15 +239,45 @@
 
 def plain_terms(here, high, low, right, left, grads):
     n, rank = right.shape[:2]
+    rows = grads.shape[1]
     core = here & 1
     sources = [((here - core) ^ offset) + c for offset, c in row_offsets(n)]
     grads = jnp.concatenate([lax.dynamic_index_in_dim(grads, source, keepdims=False) for source in sources])
-    outs = []
-    for which in (core, 1 - core):
-        some = lambda x: pick(which, *jnp.moveaxis(x.reshape(n // 2, 2, rank, -1), 1, 0)).reshape(n // 2 * rank, -1)
-        some_right, some_left = some(right), some(left)
-        outs.append(jnp.concatenate([nt_dot(high, some_right) + nt_dot(low, some_right), nt_dot(grads, some_left)], 1))
-    return outs
+    right, left = right.reshape(n * rank, -1), left.reshape(n * rank, -1)
+    both = jnp.concatenate([nt_dot(high, right) + nt_dot(low, right), nt_dot(grads, left)], 1)
+    both = both.reshape(n // 2, 2, rows, -1)
+    outs = pick(core, both[:, 0], both[:, 1]), pick(core, both[:, 1], both[:, 0])
+    return [out.reshape(n // 2 * rows, -1) for out in outs]
+
+
+def spread(wide, n):
+    query = lax.broadcasted_iota(jnp.int32, (wide, n), 0) // (wide // n)
+    return (query == lax.broadcasted_iota(jnp.int32, (wide, n), 1)).astype(F32)
+
+
+def score_kernel(n, right_ref, other_right_ref, left_ref, other_left_ref, out_ref):
+    rows, wide = other_right_ref.shape
+    products = (right_ref[:rows] + other_right_ref[...]) * (left_ref[:rows] + other_left_ref[...])
+    out_ref[...] = jnp.dot(
+        products, spread(wide, n), precision=lax.Precision.HIGHEST, preferred_element_type=F32
+    )
+
+
+def score(n, right, other_right, left, other_left):
+    whole = pl.BlockSpec(memory_space=pltpu.VMEM)
+    return pl.pallas_call(
+        functools.partial(score_kernel, n),
+        in_specs=[whole] * 4,
+        out_specs=whole,
+        out_shape=jax.ShapeDtypeStruct((other_right.shape[0], n), F32),
+        compiler_params=pltpu.CompilerParams(vmem_limit_bytes=8 * 2**20),
+        name="score",
+    )(right, other_right, left, other_left)
+
+
+def halve(sums, bit):
+    half = sums.shape[0] // 2
+    return sums[:half] + swap(sums[half:], bit)
 
 
 def body(tokens, grad_out, gate_weight, up_weight, query_left, query_right):
@@ -252,14 +293,16 @@
     lay = Layout(n, cols, width // n, own, rank)
     fits = lay.fits(lax.axis_size("groups"))
 
-    chip = chip_rows(tokens, core)
+    plane = lax.axis_index("groups") & 1
+    also = ()
+    if fits:
+        split, rest = also = pack(lay, plane, right_own, left_own, grad_out)
+    chip = chip_rows(tokens, core, also)
     blocks = {0: chip}
     for k in range(1, planes):
         blocks[k] = swap(chip, 4 * k)
 
     if fits:
-        plane = lax.axis_index("groups") & 1
-        split, rest = pack(lay, plane, right_own, left_own, grad_out)
         split = trade(after(split, blocks[1]))
         rest = trade(after(rest, *blocks.values()))
         groups = lax.axis_size("groups")
@@ -271,23 +314,26 @@
     own_half, other_half = group_rows(blocks, planes)
     if fits:
         high, low = hidden_parts(core, own_half, other_half, gate_weight, up_weight)
-        keep, send = terms(lay, here, plane, high, low, split, twin, rest)
-    else:
-        high, low = plain_hidden(core, own_half, other_half, gate_weight, up_weight)
-        keep, send = plain_terms(here, high, low, right_all, left_all, grad_all)
+        keep, send, keep_left, send_left = terms(lay, here, plane, high, low, split, twin, rest)
+        right, left = keep + swap(send, 1), keep_left + swap(send_left, 1)
+        right, left = halve(right, 2), halve(left, 4)
+        right, left = halve(right, 4), halve(left, 2)
+        bit = 8
+        while 2 * bit < n:
+            right, left = halve(right, bit), halve(left, bit)
+            bit *= 2
+        return score(n, right, swap(right[own:], bit), left, swap(left[own:], bit))
+
+    high, low = plain_hidden(core, own_half, other_half, gate_weight, up_weight)
+    keep, send = plain_terms(here, high, low, right_all, left_all, grad_all)
 
     sums = keep + swap(send, 1)
     bit = 2
     while bit < n:
-        half = sums.shape[0] // 2
-        sums = sums[:half] + swap(sums[half:], bit)
+        sums = halve(sums, bit)
         bit *= 2
-
-    wide = n // 2 * rank
-    spread = lax.broadcasted_iota(jnp.int32, (wide, n), 0) // rank * 2 + core
-    spread = (spread == lax.broadcasted_iota(jnp.int32, (wide, n), 1)).astype(F32)
-    scores = jnp.dot(sums[:, :wide] * sums[:, wide:], spread, precision=lax.Precision.HIGHEST)
-    return pick(core, scores[:own], scores[own:]) + swap(pick(core, scores[own:], scores[:own]), 1)
+    wide = n * rank
+    return jnp.dot(sums[:, :wide] * sums[:, wide:], spread(wide, n), precision=lax.Precision.HIGHEST)
 
 
 def solution(mesh):

time: 72 us -> 68.1 us (0.946)
  waiting for transfers between devices: 28.3 us -> 23 us
  starting transfers between devices: 24.7 us -> 28.8 us
  local copies, waits for them, and re-layouts: 3.79 us -> 0.09 us
  Pallas kernels: 12.7 us -> 14.4 us
    ppermute x11 -> x14, waiting for transfers between devices: 16 us -> 10.6 us  [swap(): return lax.ppermute(x, AXIS, [(i, i ^ bit) for i in range(n)])]
    unnamed x9 -> x3, local copies, waits for them, and re-layouts: 3.06 us -> 0.02 us
    ppermute x11 -> x14, starting transfers between devices: 13.5 us -> 16.5 us  [swap(): return lax.ppermute(x, AXIS, [(i, i ^ bit) for i in range(n)])]
    all_to_all x2, starting transfers between devices: 9.74 us -> 10.7 us  [trade(): return lax.all_to_all(x, AXIS, split_axis=0, concat_axis=0, tiled=True)]
    pallas_call x0 -> x1, Pallas kernels: none -> 0.85 us  [score(): pl.pallas_call(functools.partial(score_kernel, n), in_specs=[whole] * 4,...]
    pallas_call x1, Pallas kernels: 1.49 us -> 2.32 us  [pack(): pl.pallas_call(functools.partial(pack_kernel, lay), in_specs=[pl.BlockSpe...]
  transfers between devices with their start and end apart: 14 -> 17, of which waited for: 9 -> 11; matrix products, arithmetic and copies ran while one was open for 0% -> 0% of each run, Pallas kernels for 16% -> 18%
where the time goes in v3:
time: 68.1 us; the launch traced here: 67.6 us
  starting transfers between devices  28.8 us (42%)
  waiting for transfers between devices  23 us (34%)
  Pallas kernels  14.4 us (21%)
  other arithmetic  1.15 us (2%)
    ppermute x14, starting transfers between devices, swap(): return lax.ppermute(x, AXIS, [(i, i ^ bit) for i in range(n)])  16.5 us
    all_to_all x2, waiting for transfers between devices, trade(): return lax.all_to_all(x, AXIS, split_axis=0, concat_axis=0, tiled=True)  12.3 us
    all_to_all x2, starting transfers between devices, trade(): return lax.all_to_all(x, AXIS, split_axis=0, concat_axis=0, tiled=True)  10.7 us
    ppermute x14, waiting for transfers between devices, swap(): return lax.ppermute(x, AXIS, [(i, i ^ bit) for i in range(n)])  10.6 us
    pallas_call x1, Pallas kernels, hidden_parts(): pl.pallas_call(functools.partial(hidden_kernel, steps), grid_spec=pltpu.P...  9.85 us
    pallas_call x1, Pallas kernels, pack(): pl.pallas_call(functools.partial(pack_kernel, lay), in_specs=[pl.BlockSpe...  2.32 us
    ppermute x1, starting transfers between devices, body(): twin = lax.ppermute(split, 'groups', [(g, g ^ 1) for g in range(groups)])  1.49 us
    pallas_call x1, Pallas kernels, terms(): pl.pallas_call(functools.partial(term_kernel, lay), in_specs=[pl.BlockSpe...  1.39 us
  transfers between devices with their start and end apart: 17, of which 11 were waited for; matrix products, arithmetic and copies ran while one was open for 0% of the time, Pallas kernels for 18%

profile of v3, /device:TPU:0, one launch (start us, length us, event | category | flops | bytes accessed | tf_op | source)
XLA Modules:
  0.0 67.6 jit_solution(5089580303385183688)
XLA Ops:
  0.0 0.9 %broadcast_select_fusion = (bf16[12,2048]{1,0:T(8,128)(2,1)S(1)}, bf16[12,2048]{1,0:T(8,128)(2,1)S(1)}) fusion(pred[]{:T(512)S(6)} %eq.2, bf16[12,4096]{1,0:T(8,128)(2,1)} %param.6), kind=kLoop, calls=%fused_computation.4 | loop fusion | flops 49152 | bytes 196609 | tf_op jit(solution)/shard_map/jit(_where)/select_n | solution.py:23
  0.9 0.5 collective-permute-start
  1.4 2.3 %pack.1 = (bf16[16,32,384]{2,1,0:T(8,128)(2,1)}, bf16[16,32,512]{2,1,0:T(8,128)(2,1)}) custom-call(s32[1]{0:T(128)} %bitcast.1.plane_ref, bf16[32,14336]{1,0:T(8,128)(2,1)} %bitcast.9, bf16[32,4096]{1,0:T(8,128)(2,1)} %bitcast.10, bf16[12,4096]{1,0:T(8,128)(2,1)} %grad_hbm.1), custom_call_target="tpu_custom_call" | custom-call | flops 1000 | bytes 1000 | tf_op jit(solution)/shard_map/pack/pallas_call | solution.py:119
  3.7 0.0 collective-permute-done
  3.7 0.1 constant_dynamic-update-slice_fusion.4
  3.8 2.7 %collective-permute-start.2 = (bf16[24,2048]{1,0:T(8,128)(2,1)S(1)}, bf16[24,2048]{1,0:T(8,128)(2,1)S(1)}, u32[]{:S(2)}, u32[]{:S(2)}) collective-permute-start(bf16[24,2048]{1,0:T(8,128)(2,1)S(1)} %get-tuple-element.28), channel_id=1, source_target_pairs={{0,4},{1,5},{2,6},{3,7},{4,0},{5,1},{6,2},{7,3},{8,12},{9,13},{10,... | collective-permute-start | bytes 294920 | tf_op jit(solution)/shard_map/ppermute | solution.py:19
  6.5 2.6 %collective-permute-start.1 = (bf16[24,2048]{1,0:T(8,128)(2,1)S(1)}, bf16[24,2048]{1,0:T(8,128)(2,1)S(1)}, u32[]{:S(2)}, u32[]{:S(2)}) collective-permute-start(bf16[24,2048]{1,0:T(8,128)(2,1)S(1)} %get-tuple-element.28), channel_id=1, source_target_pairs={{0,8},{1,9},{2,10},{3,11},{4,12},{5,13},{6,14},{7,15},{8,0},{9,1},... | collective-permute-start | bytes 294920 | tf_op jit(solution)/shard_map/ppermute | solution.py:19
  9.1 0.0 collective-permute-start.3
  9.1 0.9 %collective-permute-done.2 = bf16[24,2048]{1,0:T(8,128)(2,1)S(1)} collective-permute-done((bf16[24,2048]{1,0:T(8,128)(2,1)S(1)}, bf16[24,2048]{1,0:T(8,128)(2,1)S(1)}, u32[]{:S(2)}, u32[]{:S(2)}) %collective-permute-start.2) | collective-permute-done | bytes 98336 | tf_op jit(solution)/shard_map/ppermute | solution.py:19
  9.9 7.2 %all-to-all-start = ((bf16[16,32,384]{2,1,0:T(8,128)(2,1)}), bf16[16,32,384]{2,1,0:T(8,128)(2,1)S(1)}, u32[]{:S(2)}, u32[]{:S(2)}) async-start(bf16[16,32,384]{2,1,0:T(8,128)(2,1)} %get-tuple-element.21), calls=%async_computation | async-start | bytes 786432 | tf_op jit(solution)/shard_map/all_to_all | solution.py:31
  17.1 0.1 collective-permute-done.1
  17.2 0.0 collective-permute-done.3
  17.2 1.9 %collective-permute-start.4 = (bf16[96,2048]{1,0:T(8,128)(2,1)S(1)}, bf16[96,2048]{1,0:T(8,128)(2,1)S(1)}, u32[]{:S(2)}, u32[]{:S(2)}) collective-permute-start(bf16[96,2048]{1,0:T(8,128)(2,1)S(1)} %pad_maximum_fusion), channel_id=1, source_target_pairs={{0,2},{1,3},{2,0},{3,1},{4,6},{5,7},{6,4},{7,5},{8,10},{9,11},{10,... | collective-permute-start | bytes 1179656 | tf_op jit(solution)/shard_map/ppermute | solution.py:19
  19.2 10.1 %all-to-all-done.split_ref = bf16[16,32,384]{2,1,0:T(8,128)(2,1)S(1)} async-done(((bf16[16,32,384]{2,1,0:T(8,128)(2,1)}), bf16[16,32,384]{2,1,0:T(8,128)(2,1)S(1)}, u32[]{:S(2)}, u32[]{:S(2)}) %all-to-all-start) | async-done | bytes 393248 | tf_op jit(solution)/shard_map/all_to_all | solution.py:31
  29.3 3.6 %all-to-all-start.1 = ((bf16[16,32,512]{2,1,0:T(8,128)(2,1)}), bf16[16,32,512]{2,1,0:T(8,128)(2,1)S(1)}, u32[]{:S(2)}, u32[]{:S(2)}) async-start(bf16[16,32,512]{2,1,0:T(8,128)(2,1)} %get-tuple-element.22), calls=%async_computation.1 | async-start | bytes 1048576 | tf_op jit(solution)/shard_map/all_to_all | solution.py:31
  32.9 0.0 collective-permute-done.4
  33.0 0.4 collective-permute-start.5
  33.4 1.5 %collective-permute-start.6 = (bf16[16,32,384]{2,1,0:T(8,128)(2,1)S(1)}, bf16[16,32,384]{2,1,0:T(8,128)(2,1)S(1)}, u32[]{:S(2)}, u32[]{:S(2)}) collective-permute-start(bf16[16,32,384]{2,1,0:T(8,128)(2,1)S(1)} %all-to-all-done.split_ref), channel_id=1, source_target_pairs={{0,16},{16,0},{1,17},{17,1},{2,18},{18,2},{3,19},{19,3},{4,20},{20... | collective-permute-start | bytes 1179656 | tf_op jit(solution)/shard_map/ppermute | solution.py:309
  34.9 0.1 pad_add_fusion.at_ref
  34.9 0.4 collective-permute-done.5.other_ref
  35.3 9.8 %hidden.1 = (bf16[192,896]{1,0:T(8,128)(2,1)S(1)}, bf16[192,896]{1,0:T(8,128)(2,1)S(1)}) custom-call(s32[1]{0:T(128)} %bitcast.2.core_ref, bf16[192,2048]{1,0:T(8,128)(2,1)S(1)} %constant_dynamic-update-slice_fusion.own_ref, bf16[192,2048]{1,0:T(8,128)(2,1)S(1)} %collective-permute-done.5.other_ref, bf16[4096,896]{1,0:T(8,128)(2,1)} %gate_ref.1, ...), custom_call_target="tpu_custom_call" | custom-call | flops 1000 | bytes 1000 | tf_op jit(solution)/shard_map/hidden/pallas_call | solution.py:166
  45.2 2.2 %all-to-all-done.1.rest_ref = bf16[16,32,512]{2,1,0:T(8,128)(2,1)S(1)} async-done(((bf16[16,32,512]{2,1,0:T(8,128)(2,1)}), bf16[16,32,512]{2,1,0:T(8,128)(2,1)S(1)}, u32[]{:S(2)}, u32[]{:S(2)}) %all-to-all-start.1) | async-done | bytes 524320 | tf_op jit(solution)/shard_map/all_to_all | solution.py:31
  47.3 0.0 collective-permute-done.6.twin_ref
  47.3 1.4 %terms.1 = (f32[96,512]{1,0:T(8,128)S(1)}, f32[96,512]{1,0:T(8,128)S(1)}, f32[96,512]{1,0:T(8,128)S(1)}, f32[96,512]{1,0:T(8,128)S(1)}) custom-call(s32[2]{0:T(128)S(1)} %pad_add_fusion.at_ref, bf16[192,896]{1,0:T(8,128)(2,1)S(1)} %get-tuple-element.19.high_ref, bf16[192,896]{1,0:T(8,128)(2,1)S(1)} %get-tuple-element.20.low_ref, ...), custom_call_target="tpu_custom_call" | custom-call | tf_op jit(solution)/shard_map/terms/pallas_call | solution.py:225
  48.7 0.1 collective-permute-start.11
  48.8 0.5 collective-permute-start.7
  49.3 0.9 %collective-permute-done.11 = f32[96,512]{1,0:T(8,128)S(1)} collective-permute-done((f32[96,512]{1,0:T(8,128)S(1)}, f32[96,512]{1,0:T(8,128)S(1)}, u32[]{:S(2)}, u32[]{:S(2)}) %collective-permute-start.11) | collective-permute-done | bytes 196640 | tf_op jit(solution)/shard_map/ppermute | solution.py:19
  50.3 1.5 %collective-permute-start.12 = (f32[48,512]{1,0:T(8,128)S(1)}, f32[48,512]{1,0:T(8,128)S(1)}, u32[]{:S(2)}, u32[]{:S(2)}) collective-permute-start(f32[48,512]{1,0:T(8,128)S(1)} %slice.56), channel_id=1, source_target_pairs={{0,4},{1,5},{2,6},{3,7},{4,0},{5,1},{6,2},{7,3},{8,12},{9,13},{10,... | collective-permute-start | bytes 294920 | tf_op jit(solution)/shard_map/ppermute | solution.py:19
  51.7 0.0 collective-permute-done.7
  51.8 1.0 %collective-permute-start.8 = (f32[48,512]{1,0:T(8,128)S(1)}, f32[48,512]{1,0:T(8,128)S(1)}, u32[]{:S(2)}, u32[]{:S(2)}) collective-permute-start(f32[48,512]{1,0:T(8,128)S(1)} %slice.51), channel_id=1, source_target_pairs={{0,2},{1,3},{2,0},{3,1},{4,6},{5,7},{6,4},{7,5},{8,10},{9,11},{10,... | collective-permute-start | bytes 294920 | tf_op jit(solution)/shard_map/ppermute | solution.py:19
  52.8 2.4 %collective-permute-done.12 = f32[48,512]{1,0:T(8,128)S(1)} collective-permute-done((f32[48,512]{1,0:T(8,128)S(1)}, f32[48,512]{1,0:T(8,128)S(1)}, u32[]{:S(2)}, u32[]{:S(2)}) %collective-permute-start.12) | collective-permute-done | bytes 98336 | tf_op jit(solution)/shard_map/ppermute | solution.py:19
  55.2 1.1 %collective-permute-start.13 = (f32[24,512]{1,0:T(8,128)S(1)}, f32[24,512]{1,0:T(8,128)S(1)}, u32[]{:S(2)}, u32[]{:S(2)}) collective-permute-start(f32[24,512]{1,0:T(8,128)S(1)} %slice.58), channel_id=1, source_target_pairs={{0,2},{1,3},{2,0},{3,1},{4,6},{5,7},{6,4},{7,5},{8,10},{9,11},{10,... | collective-permute-start | bytes 147464 | tf_op jit(solution)/shard_map/ppermute | solution.py:19
  56.3 0.3 collective-permute-done.8
  56.7 1.2 %collective-permute-start.9 = (f32[24,512]{1,0:T(8,128)S(1)}, f32[24,512]{1,0:T(8,128)S(1)}, u32[]{:S(2)}, u32[]{:S(2)}) collective-permute-start(f32[24,512]{1,0:T(8,128)S(1)} %slice.53), channel_id=1, source_target_pairs={{0,4},{1,5},{2,6},{3,7},{4,0},{5,1},{6,2},{7,3},{8,12},{9,13},{10,... | collective-permute-start | bytes 147464 | tf_op jit(solution)/shard_map/ppermute | solution.py:19
  57.9 1.5 %collective-permute-done.13 = f32[24,512]{1,0:T(8,128)S(1)} collective-permute-done((f32[24,512]{1,0:T(8,128)S(1)}, f32[24,512]{1,0:T(8,128)S(1)}, u32[]{:S(2)}, u32[]{:S(2)}) %collective-permute-start.13) | collective-permute-done | bytes 49184 | tf_op jit(solution)/shard_map/ppermute | solution.py:19
  59.4 2.3 %collective-permute-start.14 = (f32[12,512]{1,0:T(8,128)S(1)}, f32[12,512]{1,0:T(8,128)S(1)}, u32[]{:S(2)}, u32[]{:S(2)}) collective-permute-start(f32[12,512]{1,0:T(8,128)S(1)} %slice.59), channel_id=1, source_target_pairs={{0,8},{1,9},{2,10},{3,11},{4,12},{5,13},{6,14},{7,15},{8,0},{9,1},... | collective-permute-start | bytes 73736 | tf_op jit(solution)/shard_map/ppermute | solution.py:19
  61.7 0.0 collective-permute-done.9
  61.8 0.7 %collective-permute-start.10 = (f32[12,512]{1,0:T(8,128)S(1)}, f32[12,512]{1,0:T(8,128)S(1)}, u32[]{:S(2)}, u32[]{:S(2)}) collective-permute-start(f32[12,512]{1,0:T(8,128)S(1)} %slice.54), channel_id=1, source_target_pairs={{0,8},{1,9},{2,10},{3,11},{4,12},{5,13},{6,14},{7,15},{8,0},{9,1},... | collective-permute-start | bytes 73736 | tf_op jit(solution)/shard_map/ppermute | solution.py:19
  62.5 1.8 %collective-permute-done.14.other_left_ref = f32[12,512]{1,0:T(8,128)S(1)} collective-permute-done((f32[12,512]{1,0:T(8,128)S(1)}, f32[12,512]{1,0:T(8,128)S(1)}, u32[]{:S(2)}, u32[]{:S(2)}) %collective-permute-start.14) | collective-permute-done | bytes 24608 | tf_op jit(solution)/shard_map/ppermute | solution.py:19
  64.3 2.4 %collective-permute-done.10.other_right_ref = f32[12,512]{1,0:T(8,128)S(1)} collective-permute-done((f32[12,512]{1,0:T(8,128)S(1)}, f32[12,512]{1,0:T(8,128)S(1)}, u32[]{:S(2)}, u32[]{:S(2)}) %collective-permute-start.10) | collective-permute-done | bytes 24608 | tf_op jit(solution)/shard_map/ppermute | solution.py:19
  66.7 0.9 %score.1 = f32[12,16]{1,0:T(8,128)} custom-call(f32[24,512]{1,0:T(8,128)S(1)} %slice_add_fusion.3.right_ref, f32[12,512]{1,0:T(8,128)S(1)} %collective-permute-done.10.other_right_ref, f32[24,512]{1,0:T(8,128)S(1)} %slice_add_fusion.2.left_ref, f32[12,512]{1,0:T(8,128)S(1)} %collective-permute-done.14.other_left_ref), custom_call_target="tpu_custom_call" | custom-call | tf_op jit(solution)/shard_map/score/pallas_call | solution.py:268
  (17 shorter events, 0.2 us)
Async XLA Ops:
  0.9 2.9 %collective-permute-start = (bf16[12,2048]{1,0:T(8,128)(2,1)S(1)}, bf16[12,2048]{1,0:T(8,128)(2,1)S(1)}, u32[]{:S(2)}, u32[]{:S(2)}) collective-permute-start(bf16[12,2048]{1,0:T(8,128)(2,1)S(1)} %get-tuple-element.29), channel_id=1, source_target_pairs={{0,1},{1,0},{2,3},{3,2},{4,5},{5,4},{6,7},{7,6},{8,9},{9,8},{10,11... | collective-permute-start | bytes 147464 | tf_op jit(solution)/shard_map/ppermute | solution.py:19
  3.8 6.1 %collective-permute-start.2 = (bf16[24,2048]{1,0:T(8,128)(2,1)S(1)}, bf16[24,2048]{1,0:T(8,128)(2,1)S(1)}, u32[]{:S(2)}, u32[]{:S(2)}) collective-permute-start(bf16[24,2048]{1,0:T(8,128)(2,1)S(1)} %get-tuple-element.28), channel_id=1, source_target_pairs={{0,4},{1,5},{2,6},{3,7},{4,0},{5,1},{6,2},{7,3},{8,12},{9,13},{10,... | collective-permute-start | bytes 294920 | tf_op jit(solution)/shard_map/ppermute | solution.py:19
  6.5 10.7 %collective-permute-start.1 = (bf16[24,2048]{1,0:T(8,128)(2,1)S(1)}, bf16[24,2048]{1,0:T(8,128)(2,1)S(1)}, u32[]{:S(2)}, u32[]{:S(2)}) collective-permute-start(bf16[24,2048]{1,0:T(8,128)(2,1)S(1)} %get-tuple-element.28), channel_id=1, source_target_pairs={{0,8},{1,9},{2,10},{3,11},{4,12},{5,13},{6,14},{7,15},{8,0},{9,1},... | collective-permute-start | bytes 294920 | tf_op jit(solution)/shard_map/ppermute | solution.py:19
  9.1 8.2 %collective-permute-start.3 = (bf16[24,2048]{1,0:T(8,128)(2,1)S(1)}, bf16[24,2048]{1,0:T(8,128)(2,1)S(1)}, u32[]{:S(2)}, u32[]{:S(2)}) collective-permute-start(bf16[24,2048]{1,0:T(8,128)(2,1)S(1)} %get-tuple-element.28), channel_id=1, source_target_pairs={{0,12},{1,13},{2,14},{3,15},{4,8},{5,9},{6,10},{7,11},{8,4},{9,5},... | collective-permute-start | bytes 294920 | tf_op jit(solution)/shard_map/ppermute | solution.py:19
  9.9 19.4 %all-to-all-start = ((bf16[16,32,384]{2,1,0:T(8,128)(2,1)}), bf16[16,32,384]{2,1,0:T(8,128)(2,1)S(1)}, u32[]{:S(2)}, u32[]{:S(2)}) async-start(bf16[16,32,384]{2,1,0:T(8,128)(2,1)} %get-tuple-element.21), calls=%async_computation | async-start | bytes 786432 | tf_op jit(solution)/shard_map/all_to_all | solution.py:31
  17.2 15.7 %collective-permute-start.4 = (bf16[96,2048]{1,0:T(8,128)(2,1)S(1)}, bf16[96,2048]{1,0:T(8,128)(2,1)S(1)}, u32[]{:S(2)}, u32[]{:S(2)}) collective-permute-start(bf16[96,2048]{1,0:T(8,128)(2,1)S(1)} %pad_maximum_fusion), channel_id=1, source_target_pairs={{0,2},{1,3},{2,0},{3,1},{4,6},{5,7},{6,4},{7,5},{8,10},{9,11},{10,... | collective-permute-start | bytes 1179656 | tf_op jit(solution)/shard_map/ppermute | solution.py:19
  29.3 18.0 %all-to-all-start.1 = ((bf16[16,32,512]{2,1,0:T(8,128)(2,1)}), bf16[16,32,512]{2,1,0:T(8,128)(2,1)S(1)}, u32[]{:S(2)}, u32[]{:S(2)}) async-start(bf16[16,32,512]{2,1,0:T(8,128)(2,1)} %get-tuple-element.22), calls=%async_computation.1 | async-start | bytes 1048576 | tf_op jit(solution)/shard_map/all_to_all | solution.py:31
  33.0 2.4 %collective-permute-start.5 = (bf16[192,2048]{1,0:T(8,128)(2,1)S(1)}, bf16[192,2048]{1,0:T(8,128)(2,1)S(1)}, u32[]{:S(2)}, u32[]{:S(2)}) collective-permute-start(bf16[192,2048]{1,0:T(8,128)(2,1)S(1)} %constant_dynamic-update-slice_fusion.own_ref), channel_id=1, source_target_pairs={{0,1},{1,0},{2,3},{3,2},{4,5},{5,4},{6,7},{7,6},{8,9},{9,8},{10,11... | collective-permute-start | bytes 2359304 | tf_op jit(solution)/shard_map/ppermute | solution.py:19
  33.4 14.0 %collective-permute-start.6 = (bf16[16,32,384]{2,1,0:T(8,128)(2,1)S(1)}, bf16[16,32,384]{2,1,0:T(8,128)(2,1)S(1)}, u32[]{:S(2)}, u32[]{:S(2)}) collective-permute-start(bf16[16,32,384]{2,1,0:T(8,128)(2,1)S(1)} %all-to-all-done.split_ref), channel_id=1, source_target_pairs={{0,16},{16,0},{1,17},{17,1},{2,18},{18,2},{3,19},{19,3},{4,20},{20... | collective-permute-start | bytes 1179656 | tf_op jit(solution)/shard_map/ppermute | solution.py:309
  48.7 1.5 %collective-permute-start.11 = (f32[96,512]{1,0:T(8,128)S(1)}, f32[96,512]{1,0:T(8,128)S(1)}, u32[]{:S(2)}, u32[]{:S(2)}) collective-permute-start(f32[96,512]{1,0:T(8,128)S(1)} %get-tuple-element.26), channel_id=1, source_target_pairs={{0,1},{1,0},{2,3},{3,2},{4,5},{5,4},{6,7},{7,6},{8,9},{9,8},{10,11... | collective-permute-start | bytes 589832 | tf_op jit(solution)/shard_map/ppermute | solution.py:19
  48.8 2.9 %collective-permute-start.7 = (f32[96,512]{1,0:T(8,128)S(1)}, f32[96,512]{1,0:T(8,128)S(1)}, u32[]{:S(2)}, u32[]{:S(2)}) collective-permute-start(f32[96,512]{1,0:T(8,128)S(1)} %get-tuple-element.24), channel_id=1, source_target_pairs={{0,1},{1,0},{2,3},{3,2},{4,5},{5,4},{6,7},{7,6},{8,9},{9,8},{10,11... | collective-permute-start | bytes 589832 | tf_op jit(solution)/shard_map/ppermute | solution.py:19
  50.3 4.9 %collective-permute-start.12 = (f32[48,512]{1,0:T(8,128)S(1)}, f32[48,512]{1,0:T(8,128)S(1)}, u32[]{:S(2)}, u32[]{:S(2)}) collective-permute-start(f32[48,512]{1,0:T(8,128)S(1)} %slice.56), channel_id=1, source_target_pairs={{0,4},{1,5},{2,6},{3,7},{4,0},{5,1},{6,2},{7,3},{8,12},{9,13},{10,... | collective-permute-start | bytes 294920 | tf_op jit(solution)/shard_map/ppermute | solution.py:19
  51.8 4.8 %collective-permute-start.8 = (f32[48,512]{1,0:T(8,128)S(1)}, f32[48,512]{1,0:T(8,128)S(1)}, u32[]{:S(2)}, u32[]{:S(2)}) collective-permute-start(f32[48,512]{1,0:T(8,128)S(1)} %slice.51), channel_id=1, source_target_pairs={{0,2},{1,3},{2,0},{3,1},{4,6},{5,7},{6,4},{7,5},{8,10},{9,11},{10,... | collective-permute-start | bytes 294920 | tf_op jit(solution)/shard_map/ppermute | solution.py:19
  55.2 4.2 %collective-permute-start.13 = (f32[24,512]{1,0:T(8,128)S(1)}, f32[24,512]{1,0:T(8,128)S(1)}, u32[]{:S(2)}, u32[]{:S(2)}) collective-permute-start(f32[24,512]{1,0:T(8,128)S(1)} %slice.58), channel_id=1, source_target_pairs={{0,2},{1,3},{2,0},{3,1},{4,6},{5,7},{6,4},{7,5},{8,10},{9,11},{10,... | collective-permute-start | bytes 147464 | tf_op jit(solution)/shard_map/ppermute | solution.py:19
  56.7 5.1 %collective-permute-start.9 = (f32[24,512]{1,0:T(8,128)S(1)}, f32[24,512]{1,0:T(8,128)S(1)}, u32[]{:S(2)}, u32[]{:S(2)}) collective-permute-start(f32[24,512]{1,0:T(8,128)S(1)} %slice.53), channel_id=1, source_target_pairs={{0,4},{1,5},{2,6},{3,7},{4,0},{5,1},{6,2},{7,3},{8,12},{9,13},{10,... | collective-permute-start | bytes 147464 | tf_op jit(solution)/shard_map/ppermute | solution.py:19
  59.4 4.9 %collective-permute-start.14 = (f32[12,512]{1,0:T(8,128)S(1)}, f32[12,512]{1,0:T(8,128)S(1)}, u32[]{:S(2)}, u32[]{:S(2)}) collective-permute-start(f32[12,512]{1,0:T(8,128)S(1)} %slice.59), channel_id=1, source_target_pairs={{0,8},{1,9},{2,10},{3,11},{4,12},{5,13},{6,14},{7,15},{8,0},{9,1},... | collective-permute-start | bytes 73736 | tf_op jit(solution)/shard_map/ppermute | solution.py:19
  61.8 5.0 %collective-permute-start.10 = (f32[12,512]{1,0:T(8,128)S(1)}, f32[12,512]{1,0:T(8,128)S(1)}, u32[]{:S(2)}, u32[]{:S(2)}) collective-permute-start(f32[12,512]{1,0:T(8,128)S(1)} %slice.54), channel_id=1, source_target_pairs={{0,8},{1,9},{2,10},{3,11},{4,12},{5,13},{6,14},{7,15},{8,0},{9,1},... | collective-permute-start | bytes 73736 | tf_op jit(solution)/shard_map/ppermute | solution.py:19

commit v4 on v3

--- a/solution.py
+++ b/solution.py
@@ -57,7 +57,7 @@
 
 
 def group_rows(blocks, planes):
-    column = jnp.concatenate([blocks[k] for k in z_order(planes)])
+    column = same(jnp.concatenate([blocks[k] for k in z_order(planes)]))
     both = jnp.concatenate([column, swap(column, 2)])
     return both, swap(both, 1)
 
@@ -131,6 +131,23 @@
     )(plane.reshape(1), right, left, grads)
 
 
+def same_kernel(x_ref, out_ref):
+    out_ref[...] = x_ref[...]
+
+
+def same(x):
+    whole = pl.BlockSpec(memory_space=pltpu.VMEM)
+    return pl.pallas_call(
+        same_kernel,
+        in_specs=[whole],
+        out_specs=whole,
+        out_shape=jax.ShapeDtypeStruct(x.shape, x.dtype),
+        compiler_params=pltpu.CompilerParams(vmem_limit_bytes=4 * 2**20),
+        cost_estimate=pl.CostEstimate(flops=10_000_000_000, bytes_accessed=1000, transcendentals=0),
+        name="same",
+    )(x)
+
+
 def hidden_kernel(steps, core_ref, own_ref, other_ref, gate_ref, up_ref, high_ref, low_ref, gate, up):
     step = pl.program_id(0)
 
@@ -159,7 +176,7 @@
 def hidden_parts(core, own, other, gate_weight, up_weight):
     rows, half = own.shape
     cols = gate_weight.shape[1]
-    steps = max(1, half // 512)
+    steps = max(1, half // 1024)
     step_rows = half // steps
     weight = pl.BlockSpec((step_rows, cols), lambda s, core_ref: ((core_ref[0] * steps + s) % (2 * steps), 0))
     out = pl.BlockSpec((rows, cols), lambda s, core_ref: (0, 0))
@@ -255,24 +272,24 @@
     return (query == lax.broadcasted_iota(jnp.int32, (wide, n), 1)).astype(F32)
 
 
-def score_kernel(n, right_ref, other_right_ref, left_ref, other_left_ref, out_ref):
-    rows, wide = other_right_ref.shape
-    products = (right_ref[:rows] + other_right_ref[...]) * (left_ref[:rows] + other_left_ref[...])
+def score_kernel(n, right_ref, left_ref, other_ref, out_ref):
+    rows, wide = other_ref.shape[0], right_ref.shape[1]
+    products = (right_ref[:rows] + other_ref[:, :wide]) * (left_ref[:rows] + other_ref[:, wide:])
     out_ref[...] = jnp.dot(
         products, spread(wide, n), precision=lax.Precision.HIGHEST, preferred_element_type=F32
     )
 
 
-def score(n, right, other_right, left, other_left):
+def score(n, right, left, other):
     whole = pl.BlockSpec(memory_space=pltpu.VMEM)
     return pl.pallas_call(
         functools.partial(score_kernel, n),
-        in_specs=[whole] * 4,
+        in_specs=[whole] * 3,
         out_specs=whole,
-        out_shape=jax.ShapeDtypeStruct((other_right.shape[0], n), F32),
+        out_shape=jax.ShapeDtypeStruct((other.shape[0], n), F32),
         compiler_params=pltpu.CompilerParams(vmem_limit_bytes=8 * 2**20),
         name="score",
-    )(right, other_right, left, other_left)
+    )(right, left, other)
 
 
 def halve(sums, bit):
@@ -303,7 +320,7 @@
         blocks[k] = swap(chip, 4 * k)
 
     if fits:
-        split = trade(after(split, blocks[1]))
+        split = trade(after(split, chip))
         rest = trade(after(rest, *blocks.values()))
         groups = lax.axis_size("groups")
         twin = lax.ppermute(split, "groups", [(g, g ^ 1) for g in range(groups)])
@@ -322,7 +339,8 @@
         while 2 * bit < n:
             right, left = halve(right, bit), halve(left, bit)
             bit *= 2
-        return score(n, right, swap(right[own:], bit), left, swap(left[own:], bit))
+        other = swap(jnp.concatenate([right[own:], left[own:]], 1), bit)
+        return score(n, right, left, other)
 
     high, low = plain_hidden(core, own_half, other_half, gate_weight, up_weight)
     keep, send = plain_terms(here, high, low, right_all, left_all, grad_all)

time: 68.1 us -> 65.5 us (0.962)
  starting transfers between devices: 28.8 us -> 25.7 us
  waiting for transfers between devices: 23 us -> 25.5 us
  Pallas kernels: 14.4 us -> 12.5 us
    ppermute x14 -> x13, starting transfers between devices: 16.5 us -> 14.5 us  [swap(): return lax.ppermute(x, AXIS, [(i, i ^ bit) for i in range(n)])]
    pallas_call x1, Pallas kernels: 9.85 us -> 7.93 us  [hidden_parts(): pl.pallas_call(functools.partial(hidden_kernel, steps), grid_spec=pltpu.P...]
    ppermute x14 -> x13, waiting for transfers between devices: 10.6 us -> 12 us  [swap(): return lax.ppermute(x, AXIS, [(i, i ^ bit) for i in range(n)])]
    all_to_all x2, waiting for transfers between devices: 12.3 us -> 13.5 us  [trade(): return lax.all_to_all(x, AXIS, split_axis=0, concat_axis=0, tiled=True)]
    all_to_all x2, starting transfers between devices: 10.7 us -> 9.73 us  [trade(): return lax.all_to_all(x, AXIS, split_axis=0, concat_axis=0, tiled=True)]
  transfers between devices with their start and end apart: 17 -> 16, of which waited for: 11 -> 10; matrix products, arithmetic and copies ran while one was open for 0% -> 0% of each run, Pallas kernels for 18% -> 16%
where the time goes in v4:
time: 65.5 us; the launch traced here: 65.1 us
  starting transfers between devices  25.7 us (39%)
  waiting for transfers between devices  25.5 us (39%)
  Pallas kernels  12.5 us (19%)
  other arithmetic  1.21 us (2%)
    ppermute x13, starting transfers between devices, swap(): return lax.ppermute(x, AXIS, [(i, i ^ bit) for i in range(n)])  14.5 us
    all_to_all x2, waiting for transfers between devices, trade(): return lax.all_to_all(x, AXIS, split_axis=0, concat_axis=0, tiled=True)  13.5 us
    ppermute x13, waiting for transfers between devices, swap(): return lax.ppermute(x, AXIS, [(i, i ^ bit) for i in range(n)])  12 us
    all_to_all x2, starting transfers between devices, trade(): return lax.all_to_all(x, AXIS, split_axis=0, concat_axis=0, tiled=True)  9.73 us
    pallas_call x1, Pallas kernels, hidden_parts(): pl.pallas_call(functools.partial(hidden_kernel, steps), grid_spec=pltpu.P...  7.93 us
    pallas_call x1, Pallas kernels, pack(): pl.pallas_call(functools.partial(pack_kernel, lay), in_specs=[pl.BlockSpe...  2.31 us
    ppermute x1, starting transfers between devices, body(): twin = lax.ppermute(split, 'groups', [(g, g ^ 1) for g in range(groups)])  1.49 us
    pallas_call x1, Pallas kernels, terms(): pl.pallas_call(functools.partial(term_kernel, lay), in_specs=[pl.BlockSpe...  1.39 us
  transfers between devices with their start and end apart: 16, of which 10 were waited for; matrix products, arithmetic and copies ran while one was open for 0% of the time, Pallas kernels for 16%

profile of v4, /device:TPU:0, one launch (start us, length us, event | category | flops | bytes accessed | tf_op | source)
XLA Modules:
  0.0 65.1 jit_solution(13250996708768544733)
XLA Ops:
  0.0 0.9 %broadcast_select_fusion.1 = (bf16[12,2048]{1,0:T(8,128)(2,1)S(1)}, bf16[12,2048]{1,0:T(8,128)(2,1)S(1)}) fusion(pred[]{:T(512)S(6)} %eq.2, bf16[12,4096]{1,0:T(8,128)(2,1)} %param.6), kind=kLoop, calls=%fused_computation.7 | loop fusion | flops 49152 | bytes 196609 | tf_op jit(solution)/shard_map/jit(_where)/select_n | solution.py:23
  0.9 0.5 collective-permute-start
  1.4 2.3 %pack.1 = (bf16[16,32,384]{2,1,0:T(8,128)(2,1)}, bf16[16,32,512]{2,1,0:T(8,128)(2,1)}) custom-call(s32[1]{0:T(128)} %bitcast.1.plane_ref, bf16[32,14336]{1,0:T(8,128)(2,1)} %bitcast.9, bf16[32,4096]{1,0:T(8,128)(2,1)} %bitcast.10, bf16[12,4096]{1,0:T(8,128)(2,1)} %grad_hbm.1), custom_call_target="tpu_custom_call" | custom-call | flops 1000 | bytes 1000 | tf_op jit(solution)/shard_map/pack/pallas_call | solution.py:119
  3.7 0.0 collective-permute-done
  3.7 0.1 maximum_select_fusion
  3.8 3.7 %collective-permute-start.1 = (bf16[24,2048]{1,0:T(8,128)(2,1)S(1)}, bf16[24,2048]{1,0:T(8,128)(2,1)S(1)}, u32[]{:S(2)}, u32[]{:S(2)}) collective-permute-start(bf16[24,2048]{1,0:T(8,128)(2,1)S(1)} %maximum_select_fusion), channel_id=1, source_target_pairs={{0,8},{1,9},{2,10},{3,11},{4,12},{5,13},{6,14},{7,15},{8,0},{9,1},... | collective-permute-start | bytes 294920 | tf_op jit(solution)/shard_map/ppermute | solution.py:19
  7.5 1.6 %collective-permute-start.2 = (bf16[24,2048]{1,0:T(8,128)(2,1)S(1)}, bf16[24,2048]{1,0:T(8,128)(2,1)S(1)}, u32[]{:S(2)}, u32[]{:S(2)}) collective-permute-start(bf16[24,2048]{1,0:T(8,128)(2,1)S(1)} %maximum_select_fusion), channel_id=1, source_target_pairs={{0,4},{1,5},{2,6},{3,7},{4,0},{5,1},{6,2},{7,3},{8,12},{9,13},{10,... | collective-permute-start | bytes 294920 | tf_op jit(solution)/shard_map/ppermute | solution.py:19
  9.0 0.0 collective-permute-start.3
  9.1 6.2 %all-to-all-start = ((bf16[16,32,384]{2,1,0:T(8,128)(2,1)}), bf16[16,32,384]{2,1,0:T(8,128)(2,1)S(1)}, u32[]{:S(2)}, u32[]{:S(2)}) async-start(bf16[16,32,384]{2,1,0:T(8,128)(2,1)} %get-tuple-element.21), calls=%async_computation | async-start | bytes 786432 | tf_op jit(solution)/shard_map/all_to_all | solution.py:31
  15.2 0.0 collective-permute-done.1
  15.2 0.0 collective-permute-done.2
  15.2 1.1 %collective-permute-done.3 = bf16[24,2048]{1,0:T(8,128)(2,1)S(1)} collective-permute-done((bf16[24,2048]{1,0:T(8,128)(2,1)S(1)}, bf16[24,2048]{1,0:T(8,128)(2,1)S(1)}, u32[]{:S(2)}, u32[]{:S(2)}) %collective-permute-start.3) | collective-permute-done | bytes 98336 | tf_op jit(solution)/shard_map/ppermute | solution.py:19
  16.4 1.6 %collective-permute-start.4 = (bf16[96,2048]{1,0:T(8,128)(2,1)S(1)}, bf16[96,2048]{1,0:T(8,128)(2,1)S(1)}, u32[]{:S(2)}, u32[]{:S(2)}) collective-permute-start(bf16[96,2048]{1,0:T(8,128)(2,1)S(1)} %same.1), channel_id=1, source_target_pairs={{0,2},{1,3},{2,0},{3,1},{4,6},{5,7},{6,4},{7,5},{8,10},{9,11},{10,... | collective-permute-start | bytes 1179656 | tf_op jit(solution)/shard_map/ppermute | solution.py:19
  18.0 9.4 %all-to-all-done.split_ref = bf16[16,32,384]{2,1,0:T(8,128)(2,1)S(1)} async-done(((bf16[16,32,384]{2,1,0:T(8,128)(2,1)}), bf16[16,32,384]{2,1,0:T(8,128)(2,1)S(1)}, u32[]{:S(2)}, u32[]{:S(2)}) %all-to-all-start) | async-done | bytes 393248 | tf_op jit(solution)/shard_map/all_to_all | solution.py:31
  27.4 3.6 %all-to-all-start.1 = ((bf16[16,32,512]{2,1,0:T(8,128)(2,1)}), bf16[16,32,512]{2,1,0:T(8,128)(2,1)S(1)}, u32[]{:S(2)}, u32[]{:S(2)}) async-start(bf16[16,32,512]{2,1,0:T(8,128)(2,1)} %get-tuple-element.22), calls=%async_computation.1 | async-start | bytes 1048576 | tf_op jit(solution)/shard_map/all_to_all | solution.py:31
  31.0 0.0 collective-permute-done.4
  31.0 0.1 pad_maximum_fusion.own_ref
  31.1 0.5 collective-permute-start.5
  31.6 1.5 %collective-permute-start.6 = (bf16[16,32,384]{2,1,0:T(8,128)(2,1)S(1)}, bf16[16,32,384]{2,1,0:T(8,128)(2,1)S(1)}, u32[]{:S(2)}, u32[]{:S(2)}) collective-permute-start(bf16[16,32,384]{2,1,0:T(8,128)(2,1)S(1)} %all-to-all-done.split_ref), channel_id=1, source_target_pairs={{0,16},{16,0},{1,17},{17,1},{2,18},{18,2},{3,19},{19,3},{4,20},{20... | collective-permute-start | bytes 1179656 | tf_op jit(solution)/shard_map/ppermute | solution.py:326
  33.1 0.1 pad_add_fusion.at_ref
  33.1 0.3 collective-permute-done.5.other_ref
  33.5 7.9 %hidden.1 = (bf16[192,896]{1,0:T(8,128)(2,1)S(1)}, bf16[192,896]{1,0:T(8,128)(2,1)S(1)}) custom-call(s32[1]{0:T(128)} %bitcast.2.core_ref, bf16[192,2048]{1,0:T(8,128)(2,1)S(1)} %pad_maximum_fusion.own_ref, bf16[192,2048]{1,0:T(8,128)(2,1)S(1)} %collective-permute-done.5.other_ref, bf16[4096,896]{1,0:T(8,128)(2,1)} %gate_ref.1, bf16[4096,896]{1,0:T(8,128)(2,1)} %up_ref.1), custom_call_target="tpu_custom_call" | custom-call | flops 1000 | bytes 1000 | tf_op jit(solution)/shard_map/hidden/pallas_call | solution.py:183
  41.4 4.1 %all-to-all-done.1.rest_ref = bf16[16,32,512]{2,1,0:T(8,128)(2,1)S(1)} async-done(((bf16[16,32,512]{2,1,0:T(8,128)(2,1)}), bf16[16,32,512]{2,1,0:T(8,128)(2,1)S(1)}, u32[]{:S(2)}, u32[]{:S(2)}) %all-to-all-start.1) | async-done | bytes 524320 | tf_op jit(solution)/shard_map/all_to_all | solution.py:31
  45.5 0.0 collective-permute-done.6.twin_ref
  45.5 1.4 %terms.1 = (f32[96,512]{1,0:T(8,128)S(1)}, f32[96,512]{1,0:T(8,128)S(1)}, f32[96,512]{1,0:T(8,128)S(1)}, f32[96,512]{1,0:T(8,128)S(1)}) custom-call(s32[2]{0:T(128)S(1)} %pad_add_fusion.at_ref, bf16[192,896]{1,0:T(8,128)(2,1)S(1)} %get-tuple-element.19.high_ref, bf16[192,896]{1,0:T(8,128)(2,1)S(1)} %get-tuple-element.20.low_ref, ...), custom_call_target="tpu_custom_call" | custom-call | tf_op jit(solution)/shard_map/terms/pallas_call | solution.py:242
  46.9 0.1 collective-permute-start.10
  47.0 0.5 collective-permute-start.7
  47.5 0.9 %collective-permute-done.10 = f32[96,512]{1,0:T(8,128)S(1)} collective-permute-done((f32[96,512]{1,0:T(8,128)S(1)}, f32[96,512]{1,0:T(8,128)S(1)}, u32[]{:S(2)}, u32[]{:S(2)}) %collective-permute-start.10) | collective-permute-done | bytes 196640 | tf_op jit(solution)/shard_map/ppermute | solution.py:19
  48.5 1.5 %collective-permute-start.11 = (f32[48,512]{1,0:T(8,128)S(1)}, f32[48,512]{1,0:T(8,128)S(1)}, u32[]{:S(2)}, u32[]{:S(2)}) collective-permute-start(f32[48,512]{1,0:T(8,128)S(1)} %slice.55), channel_id=1, source_target_pairs={{0,4},{1,5},{2,6},{3,7},{4,0},{5,1},{6,2},{7,3},{8,12},{9,13},{10,... | collective-permute-start | bytes 294920 | tf_op jit(solution)/shard_map/ppermute | solution.py:19
  49.9 0.0 collective-permute-done.7
  50.0 1.0 %collective-permute-start.8 = (f32[48,512]{1,0:T(8,128)S(1)}, f32[48,512]{1,0:T(8,128)S(1)}, u32[]{:S(2)}, u32[]{:S(2)}) collective-permute-start(f32[48,512]{1,0:T(8,128)S(1)} %slice.51), channel_id=1, source_target_pairs={{0,2},{1,3},{2,0},{3,1},{4,6},{5,7},{6,4},{7,5},{8,10},{9,11},{10,... | collective-permute-start | bytes 294920 | tf_op jit(solution)/shard_map/ppermute | solution.py:19
  51.0 2.3 %collective-permute-done.11 = f32[48,512]{1,0:T(8,128)S(1)} collective-permute-done((f32[48,512]{1,0:T(8,128)S(1)}, f32[48,512]{1,0:T(8,128)S(1)}, u32[]{:S(2)}, u32[]{:S(2)}) %collective-permute-start.11) | collective-permute-done | bytes 98336 | tf_op jit(solution)/shard_map/ppermute | solution.py:19
  53.4 1.1 %collective-permute-start.12 = (f32[24,512]{1,0:T(8,128)S(1)}, f32[24,512]{1,0:T(8,128)S(1)}, u32[]{:S(2)}, u32[]{:S(2)}) collective-permute-start(f32[24,512]{1,0:T(8,128)S(1)} %slice.57), channel_id=1, source_target_pairs={{0,2},{1,3},{2,0},{3,1},{4,6},{5,7},{6,4},{7,5},{8,10},{9,11},{10,... | collective-permute-start | bytes 147464 | tf_op jit(solution)/shard_map/ppermute | solution.py:19
  54.5 0.3 collective-permute-done.8
  54.8 1.2 %collective-permute-start.9 = (f32[24,512]{1,0:T(8,128)S(1)}, f32[24,512]{1,0:T(8,128)S(1)}, u32[]{:S(2)}, u32[]{:S(2)}) collective-permute-start(f32[24,512]{1,0:T(8,128)S(1)} %slice.53), channel_id=1, source_target_pairs={{0,4},{1,5},{2,6},{3,7},{4,0},{5,1},{6,2},{7,3},{8,12},{9,13},{10,... | collective-permute-start | bytes 147464 | tf_op jit(solution)/shard_map/ppermute | solution.py:19
  56.1 1.5 %collective-permute-done.12 = f32[24,512]{1,0:T(8,128)S(1)} collective-permute-done((f32[24,512]{1,0:T(8,128)S(1)}, f32[24,512]{1,0:T(8,128)S(1)}, u32[]{:S(2)}, u32[]{:S(2)}) %collective-permute-start.12) | collective-permute-done | bytes 49184 | tf_op jit(solution)/shard_map/ppermute | solution.py:19
  57.6 1.4 %collective-permute-done.9 = f32[24,512]{1,0:T(8,128)S(1)} collective-permute-done((f32[24,512]{1,0:T(8,128)S(1)}, f32[24,512]{1,0:T(8,128)S(1)}, u32[]{:S(2)}, u32[]{:S(2)}) %collective-permute-start.9) | collective-permute-done | bytes 49184 | tf_op jit(solution)/shard_map/ppermute | solution.py:19
  59.0 1.2 %collective-permute-start.13 = (f32[12,1024]{1,0:T(8,128)S(1)}, f32[12,1024]{1,0:T(8,128)S(1)}, u32[]{:S(2)}, u32[]{:S(2)}) collective-permute-start(f32[12,1024]{1,0:T(8,128)S(1)} %pad_maximum_fusion.2), channel_id=1, source_target_pairs={{0,8},{1,9},{2,10},{3,11},{4,12},{5,13},{6,14},{7,15},{8,0},{9,1},... | collective-permute-start | bytes 147464 | tf_op jit(solution)/shard_map/ppermute | solution.py:19
  60.3 4.0 %collective-permute-done.13.other_ref = f32[12,1024]{1,0:T(8,128)S(1)} collective-permute-done((f32[12,1024]{1,0:T(8,128)S(1)}, f32[12,1024]{1,0:T(8,128)S(1)}, u32[]{:S(2)}, u32[]{:S(2)}) %collective-permute-start.13) | collective-permute-done | bytes 49184 | tf_op jit(solution)/shard_map/ppermute | solution.py:19
  64.3 0.9 %score.1 = f32[12,16]{1,0:T(8,128)} custom-call(f32[24,512]{1,0:T(8,128)S(1)} %slice_add_fusion.3.right_ref, f32[24,512]{1,0:T(8,128)S(1)} %slice_add_fusion.2.left_ref, f32[12,1024]{1,0:T(8,128)S(1)} %collective-permute-done.13.other_ref), custom_call_target="tpu_custom_call" | custom-call | tf_op jit(solution)/shard_map/score/pallas_call | solution.py:285
  (15 shorter events, 0.2 us)
Async XLA Ops:
  0.9 2.8 %collective-permute-start = (bf16[12,2048]{1,0:T(8,128)(2,1)S(1)}, bf16[12,2048]{1,0:T(8,128)(2,1)S(1)}, u32[]{:S(2)}, u32[]{:S(2)}) collective-permute-start(bf16[12,2048]{1,0:T(8,128)(2,1)S(1)} %get-tuple-element.28), channel_id=1, source_target_pairs={{0,1},{1,0},{2,3},{3,2},{4,5},{5,4},{6,7},{7,6},{8,9},{9,8},{10,11... | collective-permute-start | bytes 147464 | tf_op jit(solution)/shard_map/ppermute | solution.py:19
  3.8 11.4 %collective-permute-start.1 = (bf16[24,2048]{1,0:T(8,128)(2,1)S(1)}, bf16[24,2048]{1,0:T(8,128)(2,1)S(1)}, u32[]{:S(2)}, u32[]{:S(2)}) collective-permute-start(bf16[24,2048]{1,0:T(8,128)(2,1)S(1)} %maximum_select_fusion), channel_id=1, source_target_pairs={{0,8},{1,9},{2,10},{3,11},{4,12},{5,13},{6,14},{7,15},{8,0},{9,1},... | collective-permute-start | bytes 294920 | tf_op jit(solution)/shard_map/ppermute | solution.py:19
  7.5 7.8 %collective-permute-start.2 = (bf16[24,2048]{1,0:T(8,128)(2,1)S(1)}, bf16[24,2048]{1,0:T(8,128)(2,1)S(1)}, u32[]{:S(2)}, u32[]{:S(2)}) collective-permute-start(bf16[24,2048]{1,0:T(8,128)(2,1)S(1)} %maximum_select_fusion), channel_id=1, source_target_pairs={{0,4},{1,5},{2,6},{3,7},{4,0},{5,1},{6,2},{7,3},{8,12},{9,13},{10,... | collective-permute-start | bytes 294920 | tf_op jit(solution)/shard_map/ppermute | solution.py:19
  9.0 7.3 %collective-permute-start.3 = (bf16[24,2048]{1,0:T(8,128)(2,1)S(1)}, bf16[24,2048]{1,0:T(8,128)(2,1)S(1)}, u32[]{:S(2)}, u32[]{:S(2)}) collective-permute-start(bf16[24,2048]{1,0:T(8,128)(2,1)S(1)} %maximum_select_fusion), channel_id=1, source_target_pairs={{0,12},{1,13},{2,14},{3,15},{4,8},{5,9},{6,10},{7,11},{8,4},{9,5},... | collective-permute-start | bytes 294920 | tf_op jit(solution)/shard_map/ppermute | solution.py:19
  9.1 18.4 %all-to-all-start = ((bf16[16,32,384]{2,1,0:T(8,128)(2,1)}), bf16[16,32,384]{2,1,0:T(8,128)(2,1)S(1)}, u32[]{:S(2)}, u32[]{:S(2)}) async-start(bf16[16,32,384]{2,1,0:T(8,128)(2,1)} %get-tuple-element.21), calls=%async_computation | async-start | bytes 786432 | tf_op jit(solution)/shard_map/all_to_all | solution.py:31
  16.4 14.6 %collective-permute-start.4 = (bf16[96,2048]{1,0:T(8,128)(2,1)S(1)}, bf16[96,2048]{1,0:T(8,128)(2,1)S(1)}, u32[]{:S(2)}, u32[]{:S(2)}) collective-permute-start(bf16[96,2048]{1,0:T(8,128)(2,1)S(1)} %same.1), channel_id=1, source_target_pairs={{0,2},{1,3},{2,0},{3,1},{4,6},{5,7},{6,4},{7,5},{8,10},{9,11},{10,... | collective-permute-start | bytes 1179656 | tf_op jit(solution)/shard_map/ppermute | solution.py:19
  27.4 18.0 %all-to-all-start.1 = ((bf16[16,32,512]{2,1,0:T(8,128)(2,1)}), bf16[16,32,512]{2,1,0:T(8,128)(2,1)S(1)}, u32[]{:S(2)}, u32[]{:S(2)}) async-start(bf16[16,32,512]{2,1,0:T(8,128)(2,1)} %get-tuple-element.22), calls=%async_computation.1 | async-start | bytes 1048576 | tf_op jit(solution)/shard_map/all_to_all | solution.py:31
  31.1 2.4 %collective-permute-start.5 = (bf16[192,2048]{1,0:T(8,128)(2,1)S(1)}, bf16[192,2048]{1,0:T(8,128)(2,1)S(1)}, u32[]{:S(2)}, u32[]{:S(2)}) collective-permute-start(bf16[192,2048]{1,0:T(8,128)(2,1)S(1)} %pad_maximum_fusion.own_ref), channel_id=1, source_target_pairs={{0,1},{1,0},{2,3},{3,2},{4,5},{5,4},{6,7},{7,6},{8,9},{9,8},{10,11... | collective-permute-start | bytes 2359304 | tf_op jit(solution)/shard_map/ppermute | solution.py:19
  31.6 13.9 %collective-permute-start.6 = (bf16[16,32,384]{2,1,0:T(8,128)(2,1)S(1)}, bf16[16,32,384]{2,1,0:T(8,128)(2,1)S(1)}, u32[]{:S(2)}, u32[]{:S(2)}) collective-permute-start(bf16[16,32,384]{2,1,0:T(8,128)(2,1)S(1)} %all-to-all-done.split_ref), channel_id=1, source_target_pairs={{0,16},{16,0},{1,17},{17,1},{2,18},{18,2},{3,19},{19,3},{4,20},{20... | collective-permute-start | bytes 1179656 | tf_op jit(solution)/shard_map/ppermute | solution.py:326
  46.9 1.5 %collective-permute-start.10 = (f32[96,512]{1,0:T(8,128)S(1)}, f32[96,512]{1,0:T(8,128)S(1)}, u32[]{:S(2)}, u32[]{:S(2)}) collective-permute-start(f32[96,512]{1,0:T(8,128)S(1)} %get-tuple-element.26), channel_id=1, source_target_pairs={{0,1},{1,0},{2,3},{3,2},{4,5},{5,4},{6,7},{7,6},{8,9},{9,8},{10,11... | collective-permute-start | bytes 589832 | tf_op jit(solution)/shard_map/ppermute | solution.py:19
  47.0 2.9 %collective-permute-start.7 = (f32[96,512]{1,0:T(8,128)S(1)}, f32[96,512]{1,0:T(8,128)S(1)}, u32[]{:S(2)}, u32[]{:S(2)}) collective-permute-start(f32[96,512]{1,0:T(8,128)S(1)} %get-tuple-element.24), channel_id=1, source_target_pairs={{0,1},{1,0},{2,3},{3,2},{4,5},{5,4},{6,7},{7,6},{8,9},{9,8},{10,11... | collective-permute-start | bytes 589832 | tf_op jit(solution)/shard_map/ppermute | solution.py:19
  48.5 4.9 %collective-permute-start.11 = (f32[48,512]{1,0:T(8,128)S(1)}, f32[48,512]{1,0:T(8,128)S(1)}, u32[]{:S(2)}, u32[]{:S(2)}) collective-permute-start(f32[48,512]{1,0:T(8,128)S(1)} %slice.55), channel_id=1, source_target_pairs={{0,4},{1,5},{2,6},{3,7},{4,0},{5,1},{6,2},{7,3},{8,12},{9,13},{10,... | collective-permute-start | bytes 294920 | tf_op jit(solution)/shard_map/ppermute | solution.py:19
  50.0 4.8 %collective-permute-start.8 = (f32[48,512]{1,0:T(8,128)S(1)}, f32[48,512]{1,0:T(8,128)S(1)}, u32[]{:S(2)}, u32[]{:S(2)}) collective-permute-start(f32[48,512]{1,0:T(8,128)S(1)} %slice.51), channel_id=1, source_target_pairs={{0,2},{1,3},{2,0},{3,1},{4,6},{5,7},{6,4},{7,5},{8,10},{9,11},{10,... | collective-permute-start | bytes 294920 | tf_op jit(solution)/shard_map/ppermute | solution.py:19
  53.4 4.2 %collective-permute-start.12 = (f32[24,512]{1,0:T(8,128)S(1)}, f32[24,512]{1,0:T(8,128)S(1)}, u32[]{:S(2)}, u32[]{:S(2)}) collective-permute-start(f32[24,512]{1,0:T(8,128)S(1)} %slice.57), channel_id=1, source_target_pairs={{0,2},{1,3},{2,0},{3,1},{4,6},{5,7},{6,4},{7,5},{8,10},{9,11},{10,... | collective-permute-start | bytes 147464 | tf_op jit(solution)/shard_map/ppermute | solution.py:19
  54.8 4.2 %collective-permute-start.9 = (f32[24,512]{1,0:T(8,128)S(1)}, f32[24,512]{1,0:T(8,128)S(1)}, u32[]{:S(2)}, u32[]{:S(2)}) collective-permute-start(f32[24,512]{1,0:T(8,128)S(1)} %slice.53), channel_id=1, source_target_pairs={{0,4},{1,5},{2,6},{3,7},{4,0},{5,1},{6,2},{7,3},{8,12},{9,13},{10,... | collective-permute-start | bytes 147464 | tf_op jit(solution)/shard_map/ppermute | solution.py:19
  59.0 5.2 %collective-permute-start.13 = (f32[12,1024]{1,0:T(8,128)S(1)}, f32[12,1024]{1,0:T(8,128)S(1)}, u32[]{:S(2)}, u32[]{:S(2)}) collective-permute-start(f32[12,1024]{1,0:T(8,128)S(1)} %pad_maximum_fusion.2), channel_id=1, source_target_pairs={{0,8},{1,9},{2,10},{3,11},{4,12},{5,13},{6,14},{7,15},{8,0},{9,1},... | collective-permute-start | bytes 147464 | tf_op jit(solution)/shard_map/ppermute | solution.py:19

commit v5 on v4

--- a/solution.py
+++ b/solution.py
@@ -91,44 +91,47 @@
         )
 
 
-def pack_kernel(lay, plane_ref, right_hbm, left_hbm, grad_hbm, split_ref, rest_ref, right_ref, left_ref, grad_ref, sems):
-    copies = [
-        pltpu.make_async_copy(source, to, sems.at[at])
-        for at, (source, to) in enumerate(((right_hbm, right_ref), (left_hbm, left_ref), (grad_hbm, grad_ref)))
-    ]
+def fetch(pairs, sems):
+    copies = [pltpu.make_async_copy(source, to, sems.at[at]) for at, (source, to) in enumerate(pairs)]
     for copy in copies:
         copy.start()
     for copy in copies:
         copy.wait()
+
+
+def split_kernel(lay, plane_ref, right_hbm, left_hbm, split_ref, right_ref, left_ref, sems):
+    fetch(((right_hbm, right_ref), (left_hbm, left_ref)), sems)
     plane = plane_ref[0]
-    cols, depth, part, common = lay.cols, lay.depth, lay.part, lay.common
     for to in range(lay.n):
-        at = pl.multiple_of(to * cols + plane * part, LANES)
-        split_ref[to, :, :part] = right_ref[:, pl.ds(at, part)]
-        at = pl.multiple_of(to * depth + plane * lay.left, LANES)
-        split_ref[to, :, part:] = left_ref[:, pl.ds(at, lay.left)]
-        rest_ref[to, :, :common] = right_ref[:, to * cols + 2 * part : (to + 1) * cols]
+        at = pl.multiple_of(to * lay.cols + plane * lay.part, LANES)
+        split_ref[to, :, : lay.part] = right_ref[:, pl.ds(at, lay.part)]
+        at = pl.multiple_of(to * lay.depth + plane * lay.left, LANES)
+        split_ref[to, :, lay.part :] = left_ref[:, pl.ds(at, lay.left)]
+
+
+def rest_kernel(lay, right_hbm, grad_hbm, rest_ref, right_ref, grad_ref, sems):
+    fetch(((right_hbm, right_ref), (grad_hbm, grad_ref)), sems)
+    cols, depth, common = lay.cols, lay.depth, lay.common
+    for to in range(lay.n):
+        rest_ref[to, :, :common] = right_ref[:, to * cols + 2 * lay.part : (to + 1) * cols]
         grad = grad_ref[:, to * depth : (to + 1) * depth].astype(F32)
         grad = jnp.concatenate([grad, jnp.zeros((PAD - lay.rows, depth), F32)]).astype(BF16)
         for piece in range(depth // LANES):
             rest_ref[to, piece * PAD : (piece + 1) * PAD, common:] = grad[:, piece * LANES : (piece + 1) * LANES]
 
 
-def pack(lay, plane, right, left, grads):
-    whole, away = pl.BlockSpec(memory_space=pltpu.VMEM), pl.BlockSpec(memory_space=pl.ANY)
-    return pl.pallas_call(
-        functools.partial(pack_kernel, lay),
-        in_specs=[pl.BlockSpec(memory_space=pltpu.SMEM), away, away, away],
-        out_specs=[whole, whole],
-        out_shape=[
-            jax.ShapeDtypeStruct((lay.n, lay.rank, lay.part + lay.left), BF16),
-            jax.ShapeDtypeStruct((lay.n, lay.rank, lay.common + LANES), BF16),
-        ],
-        scratch_shapes=[pltpu.VMEM(x.shape, BF16) for x in (right, left, grads)] + [pltpu.SemaphoreType.DMA((3,))],
+def pack(kernel, name, lay, lanes, scalars, arrays):
+    away = pl.BlockSpec(memory_space=pl.ANY)
+    return pl.pallas_call(
+        functools.partial(kernel, lay),
+        in_specs=[pl.BlockSpec(memory_space=pltpu.SMEM)] * len(scalars) + [away] * len(arrays),
+        out_specs=pl.BlockSpec(memory_space=pltpu.VMEM),
+        out_shape=jax.ShapeDtypeStruct((lay.n, lay.rank, lanes), BF16),
+        scratch_shapes=[pltpu.VMEM(x.shape, BF16) for x in arrays] + [pltpu.SemaphoreType.DMA((len(arrays),))],
         compiler_params=pltpu.CompilerParams(vmem_limit_bytes=56 * 2**20),
         cost_estimate=pl.CostEstimate(flops=1000, bytes_accessed=1000, transcendentals=0),
-        name="pack",
-    )(plane.reshape(1), right, left, grads)
+        name=name,
+    )(*scalars, *arrays)
 
 
 def same_kernel(x_ref, out_ref):
@@ -313,7 +316,8 @@
     plane = lax.axis_index("groups") & 1
     also = ()
     if fits:
-        split, rest = also = pack(lay, plane, right_own, left_own, grad_out)
+        split = pack(split_kernel, "split", lay, lay.part + lay.left, (plane.reshape(1),), (right_own, left_own))
+        also = (split,)
     chip = chip_rows(tokens, core, also)
     blocks = {0: chip}
     for k in range(1, planes):
@@ -321,7 +325,8 @@
 
     if fits:
         split = trade(after(split, chip))
-        rest = trade(after(rest, *blocks.values()))
+        late = after(grad_out, *blocks.values())
+        rest = trade(pack(rest_kernel, "rest", lay, lay.common + LANES, (), (right_own, late)))
         groups = lax.axis_size("groups")
         twin = lax.ppermute(split, "groups", [(g, g ^ 1) for g in range(groups)])
     else:

time: 65.5 us -> 65.2 us (level)
  waiting for transfers between devices: 25.5 us -> 23.5 us
  Pallas kernels: 12.5 us -> 14.3 us
    all_to_all x2, waiting for transfers between devices: 13.5 us -> 10.4 us  [trade(): return lax.all_to_all(x, AXIS, split_axis=0, concat_axis=0, tiled=True)]
    pallas_call x1 -> x2, Pallas kernels: 2.31 us -> 4.11 us  [pack(): pl.pallas_call(functools.partial(kernel, lay), in_specs=[pl.BlockSpec(mem...]
    ppermute x13, waiting for transfers between devices: 12 us -> 13.1 us  [swap(): return lax.ppermute(x, AXIS, [(i, i ^ bit) for i in range(n)])]
  transfers between devices with their start and end apart: 16 -> 16, of which waited for: 10 -> 11; matrix products, arithmetic and copies ran while one was open for 0% -> 0% of each run, Pallas kernels for 16% -> 19%
where the time goes in v5:
time: 65.2 us; the launch traced here: 64.8 us
  starting transfers between devices  25.6 us (39%)
  waiting for transfers between devices  23.5 us (36%)
  Pallas kernels  14.3 us (22%)
  other arithmetic  1.21 us (2%)
    ppermute x13, starting transfers between devices, swap(): return lax.ppermute(x, AXIS, [(i, i ^ bit) for i in range(n)])  14.4 us
    ppermute x13, waiting for transfers between devices, swap(): return lax.ppermute(x, AXIS, [(i, i ^ bit) for i in range(n)])  13.1 us
    all_to_all x2, waiting for transfers between devices, trade(): return lax.all_to_all(x, AXIS, split_axis=0, concat_axis=0, tiled=True)  10.4 us
    all_to_all x2, starting transfers between devices, trade(): return lax.all_to_all(x, AXIS, split_axis=0, concat_axis=0, tiled=True)  9.65 us
    pallas_call x1, Pallas kernels, hidden_parts(): pl.pallas_call(functools.partial(hidden_kernel, steps), grid_spec=pltpu.P...  7.93 us
    pallas_call x2, Pallas kernels, pack(): pl.pallas_call(functools.partial(kernel, lay), in_specs=[pl.BlockSpec(mem...  4.11 us
    ppermute x1, starting transfers between devices, body(): twin = lax.ppermute(split, 'groups', [(g, g ^ 1) for g in range(groups)])  1.49 us
    pallas_call x1, Pallas kernels, terms(): pl.pallas_call(functools.partial(term_kernel, lay), in_specs=[pl.BlockSpe...  1.39 us
  transfers between devices with their start and end apart: 16, of which 11 were waited for; matrix products, arithmetic and copies ran while one was open for 0% of the time, Pallas kernels for 19%

profile of v5, /device:TPU:0, one launch (start us, length us, event | category | flops | bytes accessed | tf_op | source)
XLA Modules:
  0.0 64.8 jit_solution(1119168991260800581)
XLA Ops:
  0.0 0.9 %broadcast_select_fusion.1 = (bf16[12,2048]{1,0:T(8,128)(2,1)S(1)}, bf16[12,2048]{1,0:T(8,128)(2,1)S(1)}) fusion(pred[]{:T(512)S(6)} %eq.2, bf16[12,4096]{1,0:T(8,128)(2,1)} %param.6), kind=kLoop, calls=%fused_computation.7 | loop fusion | flops 49152 | bytes 196609 | tf_op jit(solution)/shard_map/jit(_where)/select_n | solution.py:23
  0.9 0.5 collective-permute-start
  1.4 2.1 %split.1 = bf16[16,32,384]{2,1,0:T(8,128)(2,1)} custom-call(s32[1]{0:T(128)} %bitcast.1.plane_ref, bf16[32,14336]{1,0:T(8,128)(2,1)} %bitcast.9, bf16[32,4096]{1,0:T(8,128)(2,1)} %bitcast.11), custom_call_target="tpu_custom_call" | custom-call | flops 1000 | bytes 1000 | tf_op jit(solution)/shard_map/split/pallas_call | solution.py:125
  3.5 0.0 collective-permute-done
  3.5 0.1 maximum_select_fusion
  3.6 4.7 %collective-permute-start.3 = (bf16[24,2048]{1,0:T(8,128)(2,1)S(1)}, bf16[24,2048]{1,0:T(8,128)(2,1)S(1)}, u32[]{:S(2)}, u32[]{:S(2)}) collective-permute-start(bf16[24,2048]{1,0:T(8,128)(2,1)S(1)} %maximum_select_fusion), channel_id=1, source_target_pairs={{0,12},{1,13},{2,14},{3,15},{4,8},{5,9},{6,10},{7,11},{8,4},{9,5},... | collective-permute-start | bytes 294920 | tf_op jit(solution)/shard_map/ppermute | solution.py:19
  8.2 0.0 collective-permute-start.2
  8.2 0.6 collective-permute-start.1
  8.9 6.1 %all-to-all-start = ((bf16[16,32,384]{2,1,0:T(8,128)(2,1)}), bf16[16,32,384]{2,1,0:T(8,128)(2,1)S(1)}, u32[]{:S(2)}, u32[]{:S(2)}) async-start(bf16[16,32,384]{2,1,0:T(8,128)(2,1)} %split.1), calls=%async_computation | async-start | bytes 786432 | tf_op jit(solution)/shard_map/all_to_all | solution.py:31
  15.0 0.0 collective-permute-done.3
  15.0 0.0 collective-permute-done.2
  15.0 2.2 %collective-permute-done.1 = bf16[24,2048]{1,0:T(8,128)(2,1)S(1)} collective-permute-done((bf16[24,2048]{1,0:T(8,128)(2,1)S(1)}, bf16[24,2048]{1,0:T(8,128)(2,1)S(1)}, u32[]{:S(2)}, u32[]{:S(2)}) %collective-permute-start.1) | collective-permute-done | bytes 98336 | tf_op jit(solution)/shard_map/ppermute | solution.py:19
  17.2 1.6 %collective-permute-start.4 = (bf16[96,2048]{1,0:T(8,128)(2,1)S(1)}, bf16[96,2048]{1,0:T(8,128)(2,1)S(1)}, u32[]{:S(2)}, u32[]{:S(2)}) collective-permute-start(bf16[96,2048]{1,0:T(8,128)(2,1)S(1)} %same.1), channel_id=1, source_target_pairs={{0,2},{1,3},{2,0},{3,1},{4,6},{5,7},{6,4},{7,5},{8,10},{9,11},{10,... | collective-permute-start | bytes 1179656 | tf_op jit(solution)/shard_map/ppermute | solution.py:19
  18.8 2.0 %rest.1 = bf16[16,32,512]{2,1,0:T(8,128)(2,1)} custom-call(bf16[32,14336]{1,0:T(8,128)(2,1)} %bitcast.10, bf16[12,4096]{1,0:T(8,128)(2,1)} %grad_hbm), custom_call_target="tpu_custom_call" | custom-call | flops 1000 | bytes 1000 | tf_op jit(solution)/shard_map/rest/pallas_call | solution.py:125
  20.9 6.3 %all-to-all-done.split_ref = bf16[16,32,384]{2,1,0:T(8,128)(2,1)S(1)} async-done(((bf16[16,32,384]{2,1,0:T(8,128)(2,1)}), bf16[16,32,384]{2,1,0:T(8,128)(2,1)S(1)}, u32[]{:S(2)}, u32[]{:S(2)}) %all-to-all-start) | async-done | bytes 393248 | tf_op jit(solution)/shard_map/all_to_all | solution.py:31
  27.2 3.6 %all-to-all-start.1 = ((bf16[16,32,512]{2,1,0:T(8,128)(2,1)}), bf16[16,32,512]{2,1,0:T(8,128)(2,1)S(1)}, u32[]{:S(2)}, u32[]{:S(2)}) async-start(bf16[16,32,512]{2,1,0:T(8,128)(2,1)} %rest.1), calls=%async_computation.1 | async-start | bytes 1048576 | tf_op jit(solution)/shard_map/all_to_all | solution.py:31
  30.8 0.1 collective-permute-done.4
  30.8 0.1 pad_maximum_fusion.own_ref
  30.9 0.4 collective-permute-start.5
  31.3 1.5 %collective-permute-start.6 = (bf16[16,32,384]{2,1,0:T(8,128)(2,1)S(1)}, bf16[16,32,384]{2,1,0:T(8,128)(2,1)S(1)}, u32[]{:S(2)}, u32[]{:S(2)}) collective-permute-start(bf16[16,32,384]{2,1,0:T(8,128)(2,1)S(1)} %all-to-all-done.split_ref), channel_id=1, source_target_pairs={{0,16},{16,0},{1,17},{17,1},{2,18},{18,2},{3,19},{19,3},{4,20},{20... | collective-permute-start | bytes 1179656 | tf_op jit(solution)/shard_map/ppermute | solution.py:331
  32.8 0.1 pad_add_fusion.at_ref
  32.8 0.4 collective-permute-done.5.other_ref
  33.3 7.9 %hidden.1 = (bf16[192,896]{1,0:T(8,128)(2,1)S(1)}, bf16[192,896]{1,0:T(8,128)(2,1)S(1)}) custom-call(s32[1]{0:T(128)} %bitcast.2.core_ref, bf16[192,2048]{1,0:T(8,128)(2,1)S(1)} %pad_maximum_fusion.own_ref, bf16[192,2048]{1,0:T(8,128)(2,1)S(1)} %collective-permute-done.5.other_ref, bf16[4096,896]{1,0:T(8,128)(2,1)} %gate_ref.1, bf16[4096,896]{1,0:T(8,128)(2,1)} %up_ref.1), custom_call_target="tpu_custom_call" | custom-call | flops 1000 | bytes 1000 | tf_op jit(solution)/shard_map/hidden/pallas_call | solution.py:186
  41.2 4.0 %all-to-all-done.1.rest_ref = bf16[16,32,512]{2,1,0:T(8,128)(2,1)S(1)} async-done(((bf16[16,32,512]{2,1,0:T(8,128)(2,1)}), bf16[16,32,512]{2,1,0:T(8,128)(2,1)S(1)}, u32[]{:S(2)}, u32[]{:S(2)}) %all-to-all-start.1) | async-done | bytes 524320 | tf_op jit(solution)/shard_map/all_to_all | solution.py:31
  45.2 0.0 collective-permute-done.6.twin_ref
  45.2 1.4 %terms.1 = (f32[96,512]{1,0:T(8,128)S(1)}, f32[96,512]{1,0:T(8,128)S(1)}, f32[96,512]{1,0:T(8,128)S(1)}, f32[96,512]{1,0:T(8,128)S(1)}) custom-call(s32[2]{0:T(128)S(1)} %pad_add_fusion.at_ref, bf16[192,896]{1,0:T(8,128)(2,1)S(1)} %get-tuple-element.15.high_ref, bf16[192,896]{1,0:T(8,128)(2,1)S(1)} %get-tuple-element.16.low_ref, ...), custom_call_target="tpu_custom_call" | custom-call | tf_op jit(solution)/shard_map/terms/pallas_call | solution.py:245
  46.6 0.1 collective-permute-start.10
  46.7 0.5 collective-permute-start.7
  47.2 0.9 %collective-permute-done.10 = f32[96,512]{1,0:T(8,128)S(1)} collective-permute-done((f32[96,512]{1,0:T(8,128)S(1)}, f32[96,512]{1,0:T(8,128)S(1)}, u32[]{:S(2)}, u32[]{:S(2)}) %collective-permute-start.10) | collective-permute-done | bytes 196640 | tf_op jit(solution)/shard_map/ppermute | solution.py:19
  48.2 1.4 %collective-permute-start.11 = (f32[48,512]{1,0:T(8,128)S(1)}, f32[48,512]{1,0:T(8,128)S(1)}, u32[]{:S(2)}, u32[]{:S(2)}) collective-permute-start(f32[48,512]{1,0:T(8,128)S(1)} %slice.55), channel_id=1, source_target_pairs={{0,4},{1,5},{2,6},{3,7},{4,0},{5,1},{6,2},{7,3},{8,12},{9,13},{10,... | collective-permute-start | bytes 294920 | tf_op jit(solution)/shard_map/ppermute | solution.py:19
  49.6 0.0 collective-permute-done.7
  49.7 1.0 %collective-permute-start.8 = (f32[48,512]{1,0:T(8,128)S(1)}, f32[48,512]{1,0:T(8,128)S(1)}, u32[]{:S(2)}, u32[]{:S(2)}) collective-permute-start(f32[48,512]{1,0:T(8,128)S(1)} %slice.51), channel_id=1, source_target_pairs={{0,2},{1,3},{2,0},{3,1},{4,6},{5,7},{6,4},{7,5},{8,10},{9,11},{10,... | collective-permute-start | bytes 294920 | tf_op jit(solution)/shard_map/ppermute | solution.py:19
  50.7 2.4 %collective-permute-done.11 = f32[48,512]{1,0:T(8,128)S(1)} collective-permute-done((f32[48,512]{1,0:T(8,128)S(1)}, f32[48,512]{1,0:T(8,128)S(1)}, u32[]{:S(2)}, u32[]{:S(2)}) %collective-permute-start.11) | collective-permute-done | bytes 98336 | tf_op jit(solution)/shard_map/ppermute | solution.py:19
  53.1 1.1 %collective-permute-start.12 = (f32[24,512]{1,0:T(8,128)S(1)}, f32[24,512]{1,0:T(8,128)S(1)}, u32[]{:S(2)}, u32[]{:S(2)}) collective-permute-start(f32[24,512]{1,0:T(8,128)S(1)} %slice.57), channel_id=1, source_target_pairs={{0,2},{1,3},{2,0},{3,1},{4,6},{5,7},{6,4},{7,5},{8,10},{9,11},{10,... | collective-permute-start | bytes 147464 | tf_op jit(solution)/shard_map/ppermute | solution.py:19
  54.2 0.3 collective-permute-done.8
  54.5 1.2 %collective-permute-start.9 = (f32[24,512]{1,0:T(8,128)S(1)}, f32[24,512]{1,0:T(8,128)S(1)}, u32[]{:S(2)}, u32[]{:S(2)}) collective-permute-start(f32[24,512]{1,0:T(8,128)S(1)} %slice.53), channel_id=1, source_target_pairs={{0,4},{1,5},{2,6},{3,7},{4,0},{5,1},{6,2},{7,3},{8,12},{9,13},{10,... | collective-permute-start | bytes 147464 | tf_op jit(solution)/shard_map/ppermute | solution.py:19
  55.8 1.5 %collective-permute-done.12 = f32[24,512]{1,0:T(8,128)S(1)} collective-permute-done((f32[24,512]{1,0:T(8,128)S(1)}, f32[24,512]{1,0:T(8,128)S(1)}, u32[]{:S(2)}, u32[]{:S(2)}) %collective-permute-start.12) | collective-permute-done | bytes 49184 | tf_op jit(solution)/shard_map/ppermute | solution.py:19
  57.3 1.4 %collective-permute-done.9 = f32[24,512]{1,0:T(8,128)S(1)} collective-permute-done((f32[24,512]{1,0:T(8,128)S(1)}, f32[24,512]{1,0:T(8,128)S(1)}, u32[]{:S(2)}, u32[]{:S(2)}) %collective-permute-start.9) | collective-permute-done | bytes 49184 | tf_op jit(solution)/shard_map/ppermute | solution.py:19
  58.7 1.2 %collective-permute-start.13 = (f32[12,1024]{1,0:T(8,128)S(1)}, f32[12,1024]{1,0:T(8,128)S(1)}, u32[]{:S(2)}, u32[]{:S(2)}) collective-permute-start(f32[12,1024]{1,0:T(8,128)S(1)} %pad_maximum_fusion.2), channel_id=1, source_target_pairs={{0,8},{1,9},{2,10},{3,11},{4,12},{5,13},{6,14},{7,15},{8,0},{9,1},... | collective-permute-start | bytes 147464 | tf_op jit(solution)/shard_map/ppermute | solution.py:19
  60.0 4.0 %collective-permute-done.13.other_ref = f32[12,1024]{1,0:T(8,128)S(1)} collective-permute-done((f32[12,1024]{1,0:T(8,128)S(1)}, f32[12,1024]{1,0:T(8,128)S(1)}, u32[]{:S(2)}, u32[]{:S(2)}) %collective-permute-start.13) | collective-permute-done | bytes 49184 | tf_op jit(solution)/shard_map/ppermute | solution.py:19
  64.0 0.9 %score.1 = f32[12,16]{1,0:T(8,128)} custom-call(f32[24,512]{1,0:T(8,128)S(1)} %slice_add_fusion.3.right_ref, f32[24,512]{1,0:T(8,128)S(1)} %slice_add_fusion.2.left_ref, f32[12,1024]{1,0:T(8,128)S(1)} %collective-permute-done.13.other_ref), custom_call_target="tpu_custom_call" | custom-call | tf_op jit(solution)/shard_map/score/pallas_call | solution.py:288
  (15 shorter events, 0.2 us)
Async XLA Ops:
  0.9 2.6 %collective-permute-start = (bf16[12,2048]{1,0:T(8,128)(2,1)S(1)}, bf16[12,2048]{1,0:T(8,128)(2,1)S(1)}, u32[]{:S(2)}, u32[]{:S(2)}) collective-permute-start(bf16[12,2048]{1,0:T(8,128)(2,1)S(1)} %get-tuple-element.24), channel_id=1, source_target_pairs={{0,1},{1,0},{2,3},{3,2},{4,5},{5,4},{6,7},{7,6},{8,9},{9,8},{10,11... | collective-permute-start | bytes 147464 | tf_op jit(solution)/shard_map/ppermute | solution.py:19
  3.6 11.4 %collective-permute-start.3 = (bf16[24,2048]{1,0:T(8,128)(2,1)S(1)}, bf16[24,2048]{1,0:T(8,128)(2,1)S(1)}, u32[]{:S(2)}, u32[]{:S(2)}) collective-permute-start(bf16[24,2048]{1,0:T(8,128)(2,1)S(1)} %maximum_select_fusion), channel_id=1, source_target_pairs={{0,12},{1,13},{2,14},{3,15},{4,8},{5,9},{6,10},{7,11},{8,4},{9,5},... | collective-permute-start | bytes 294920 | tf_op jit(solution)/shard_map/ppermute | solution.py:19
  8.2 6.7 %collective-permute-start.2 = (bf16[24,2048]{1,0:T(8,128)(2,1)S(1)}, bf16[24,2048]{1,0:T(8,128)(2,1)S(1)}, u32[]{:S(2)}, u32[]{:S(2)}) collective-permute-start(bf16[24,2048]{1,0:T(8,128)(2,1)S(1)} %maximum_select_fusion), channel_id=1, source_target_pairs={{0,4},{1,5},{2,6},{3,7},{4,0},{5,1},{6,2},{7,3},{8,12},{9,13},{10,... | collective-permute-start | bytes 294920 | tf_op jit(solution)/shard_map/ppermute | solution.py:19
  8.2 8.9 %collective-permute-start.1 = (bf16[24,2048]{1,0:T(8,128)(2,1)S(1)}, bf16[24,2048]{1,0:T(8,128)(2,1)S(1)}, u32[]{:S(2)}, u32[]{:S(2)}) collective-permute-start(bf16[24,2048]{1,0:T(8,128)(2,1)S(1)} %maximum_select_fusion), channel_id=1, source_target_pairs={{0,8},{1,9},{2,10},{3,11},{4,12},{5,13},{6,14},{7,15},{8,0},{9,1},... | collective-permute-start | bytes 294920 | tf_op jit(solution)/shard_map/ppermute | solution.py:19
  8.9 18.3 %all-to-all-start = ((bf16[16,32,384]{2,1,0:T(8,128)(2,1)}), bf16[16,32,384]{2,1,0:T(8,128)(2,1)S(1)}, u32[]{:S(2)}, u32[]{:S(2)}) async-start(bf16[16,32,384]{2,1,0:T(8,128)(2,1)} %split.1), calls=%async_computation | async-start | bytes 786432 | tf_op jit(solution)/shard_map/all_to_all | solution.py:31
  17.2 13.6 %collective-permute-start.4 = (bf16[96,2048]{1,0:T(8,128)(2,1)S(1)}, bf16[96,2048]{1,0:T(8,128)(2,1)S(1)}, u32[]{:S(2)}, u32[]{:S(2)}) collective-permute-start(bf16[96,2048]{1,0:T(8,128)(2,1)S(1)} %same.1), channel_id=1, source_target_pairs={{0,2},{1,3},{2,0},{3,1},{4,6},{5,7},{6,4},{7,5},{8,10},{9,11},{10,... | collective-permute-start | bytes 1179656 | tf_op jit(solution)/shard_map/ppermute | solution.py:19
  27.2 18.0 %all-to-all-start.1 = ((bf16[16,32,512]{2,1,0:T(8,128)(2,1)}), bf16[16,32,512]{2,1,0:T(8,128)(2,1)S(1)}, u32[]{:S(2)}, u32[]{:S(2)}) async-start(bf16[16,32,512]{2,1,0:T(8,128)(2,1)} %rest.1), calls=%async_computation.1 | async-start | bytes 1048576 | tf_op jit(solution)/shard_map/all_to_all | solution.py:31
  30.9 2.4 %collective-permute-start.5 = (bf16[192,2048]{1,0:T(8,128)(2,1)S(1)}, bf16[192,2048]{1,0:T(8,128)(2,1)S(1)}, u32[]{:S(2)}, u32[]{:S(2)}) collective-permute-start(bf16[192,2048]{1,0:T(8,128)(2,1)S(1)} %pad_maximum_fusion.own_ref), channel_id=1, source_target_pairs={{0,1},{1,0},{2,3},{3,2},{4,5},{5,4},{6,7},{7,6},{8,9},{9,8},{10,11... | collective-permute-start | bytes 2359304 | tf_op jit(solution)/shard_map/ppermute | solution.py:19
  31.3 13.9 %collective-permute-start.6 = (bf16[16,32,384]{2,1,0:T(8,128)(2,1)S(1)}, bf16[16,32,384]{2,1,0:T(8,128)(2,1)S(1)}, u32[]{:S(2)}, u32[]{:S(2)}) collective-permute-start(bf16[16,32,384]{2,1,0:T(8,128)(2,1)S(1)} %all-to-all-done.split_ref), channel_id=1, source_target_pairs={{0,16},{16,0},{1,17},{17,1},{2,18},{18,2},{3,19},{19,3},{4,20},{20... | collective-permute-start | bytes 1179656 | tf_op jit(solution)/shard_map/ppermute | solution.py:331
  46.6 1.5 %collective-permute-start.10 = (f32[96,512]{1,0:T(8,128)S(1)}, f32[96,512]{1,0:T(8,128)S(1)}, u32[]{:S(2)}, u32[]{:S(2)}) collective-permute-start(f32[96,512]{1,0:T(8,128)S(1)} %get-tuple-element.22), channel_id=1, source_target_pairs={{0,1},{1,0},{2,3},{3,2},{4,5},{5,4},{6,7},{7,6},{8,9},{9,8},{10,11... | collective-permute-start | bytes 589832 | tf_op jit(solution)/shard_map/ppermute | solution.py:19
  46.7 2.9 %collective-permute-start.7 = (f32[96,512]{1,0:T(8,128)S(1)}, f32[96,512]{1,0:T(8,128)S(1)}, u32[]{:S(2)}, u32[]{:S(2)}) collective-permute-start(f32[96,512]{1,0:T(8,128)S(1)} %get-tuple-element.20), channel_id=1, source_target_pairs={{0,1},{1,0},{2,3},{3,2},{4,5},{5,4},{6,7},{7,6},{8,9},{9,8},{10,11... | collective-permute-start | bytes 589832 | tf_op jit(solution)/shard_map/ppermute | solution.py:19
  48.2 4.9 %collective-permute-start.11 = (f32[48,512]{1,0:T(8,128)S(1)}, f32[48,512]{1,0:T(8,128)S(1)}, u32[]{:S(2)}, u32[]{:S(2)}) collective-permute-start(f32[48,512]{1,0:T(8,128)S(1)} %slice.55), channel_id=1, source_target_pairs={{0,4},{1,5},{2,6},{3,7},{4,0},{5,1},{6,2},{7,3},{8,12},{9,13},{10,... | collective-permute-start | bytes 294920 | tf_op jit(solution)/shard_map/ppermute | solution.py:19
  49.7 4.8 %collective-permute-start.8 = (f32[48,512]{1,0:T(8,128)S(1)}, f32[48,512]{1,0:T(8,128)S(1)}, u32[]{:S(2)}, u32[]{:S(2)}) collective-permute-start(f32[48,512]{1,0:T(8,128)S(1)} %slice.51), channel_id=1, source_target_pairs={{0,2},{1,3},{2,0},{3,1},{4,6},{5,7},{6,4},{7,5},{8,10},{9,11},{10,... | collective-permute-start | bytes 294920 | tf_op jit(solution)/shard_map/ppermute | solution.py:19
  53.1 4.2 %collective-permute-start.12 = (f32[24,512]{1,0:T(8,128)S(1)}, f32[24,512]{1,0:T(8,128)S(1)}, u32[]{:S(2)}, u32[]{:S(2)}) collective-permute-start(f32[24,512]{1,0:T(8,128)S(1)} %slice.57), channel_id=1, source_target_pairs={{0,2},{1,3},{2,0},{3,1},{4,6},{5,7},{6,4},{7,5},{8,10},{9,11},{10,... | collective-permute-start | bytes 147464 | tf_op jit(solution)/shard_map/ppermute | solution.py:19
  54.5 4.2 %collective-permute-start.9 = (f32[24,512]{1,0:T(8,128)S(1)}, f32[24,512]{1,0:T(8,128)S(1)}, u32[]{:S(2)}, u32[]{:S(2)}) collective-permute-start(f32[24,512]{1,0:T(8,128)S(1)} %slice.53), channel_id=1, source_target_pairs={{0,4},{1,5},{2,6},{3,7},{4,0},{5,1},{6,2},{7,3},{8,12},{9,13},{10,... | collective-permute-start | bytes 147464 | tf_op jit(solution)/shard_map/ppermute | solution.py:19
  58.7 5.2 %collective-permute-start.13 = (f32[12,1024]{1,0:T(8,128)S(1)}, f32[12,1024]{1,0:T(8,128)S(1)}, u32[]{:S(2)}, u32[]{:S(2)}) collective-permute-start(f32[12,1024]{1,0:T(8,128)S(1)} %pad_maximum_fusion.2), channel_id=1, source_target_pairs={{0,8},{1,9},{2,10},{3,11},{4,12},{5,13},{6,14},{7,15},{8,0},{9,1},... | collective-permute-start | bytes 147464 | tf_op jit(solution)/shard_map/ppermute | solution.py:19
